TPU v7x, 256 devices: a whole 4x4x8 slice. The times are simulated.
256 devices in a mesh: seq: 32 (over y, x, core), tp: 8 (over z).
Axes of the slice: x: 4, y: 4, z: 8, core: 2. Of those that a mesh axis runs over, the one named last changes fastest.
Arguments:
- patches: bfloat16 [1024, 16, 1280], P('seq'), may hold values from -6 to 6
- vit_qkv: bfloat16 [3, 1280, 1280], P(None, 'seq', 'tp'), may hold values from -0.15625 to 0.15625
- vit_out: bfloat16 [1280, 1280], P('tp', 'seq'), may hold values from -0.15625 to 0.15625
- merge_weight: bfloat16 [5120, 8192], P(None, 'tp'), may hold values from -0.078125 to 0.078125
- query_key_value_weight: bfloat16 [8192, 8, 10, 128], P('seq', 'tp'), may hold values from -0.0625 to 0.0625
- adapter_down: bfloat16 [8192, 128], P('tp'), may hold values from -0.0625 to 0.0625
- adapter_up_weight: bfloat16 [128, 8, 10, 128], P(None, 'tp'), may hold values from -1.5 to 1.5
- text_embed: bfloat16 [8192, 8192], P('seq', 'tp'), may hold values from -6 to 6
- vis_count: int32 [1024], replicated, may hold values from 1 to 4, as said below
- image_session: int32 [1024], replicated, may hold values from 0 to 63, as said below
- session_slot: int32 [64], replicated, may hold values from 0 to 63, as said below
- session_tenant: int32 [64], replicated, may hold values from 0 to 7
- session_len: int32 [64], replicated, may hold values from 1 to 128, as said below
Outputs:
- attended: float32 [8192, 8192], P('seq', 'tp')
Inputs may be any that keep to these rules, and one draw needn't show every extreme that they name: `vis_count`: some image has exactly 4 merged rows. `image_session`: every session owns exactly 16 images; of the 32 images encoded by one index of seq, exactly 1 belong to the sessions of each shard. A permutation: session s lies in slot session_slot[s], on shard session_slot[s] // 2. `session_len`: each session has more rows than visual rows; some session fills its slot.
All inputs are finite; a program needn't handle non-finite values.
Results may differ from a plain program's by a relative error of at most 0.024.
Values may be sent and summed in bfloat16 or wider, within the bound.
A program may use at most 128 MiB of HBM per device.

v0:
```python
import math

import jax
import jax.numpy as jnp
from jax import lax
from jax.sharding import PartitionSpec as P

DV = 1280
HV = 16
DECODER_WIDTH = 8192
DECODER_HEAD_DIM = 128
ADAPTER_RANK = 16
IMG_DEV = 32
VMAX = 4
SESS_DEV = 2
TOK_DEV = 256
QUERY_PER_KEY = 8
SLOT = 128


EPSILON = 1e-06
ROPE_BASE = 1000000.0


def layer_norm(values):
    mean_val = jnp.mean(values, axis=-1, keepdims=True)
    centered = values - mean_val
    variance = jnp.mean(centered * centered, axis=-1, keepdims=True)
    return centered * lax.rsqrt(variance + EPSILON)


def softmax_rows(scores):
    largest = jnp.max(scores, axis=-1, keepdims=True)
    exponent = jnp.exp(scores - largest)
    return exponent / jnp.sum(exponent, axis=-1, keepdims=True)


def rotate(values, pos_float):
    half_dim = values.shape[-1] // 2
    inverse_freq = ROPE_BASE ** (
        -(jnp.arange(half_dim, dtype=jnp.float32) * 2.0 / values.shape[-1])
    )
    angles = pos_float[:, None] * inverse_freq[None, :]
    new_shape = (values.shape[0],) + (1,) * (values.ndim - 2) + (half_dim,)
    cosine = jnp.cos(angles).reshape(new_shape)
    sine_part = jnp.sin(angles).reshape(new_shape)
    first_half = values[..., :half_dim]
    second = values[..., half_dim:]
    return jnp.concatenate(
        [first_half * cosine - second * sine_part, second * cosine + first_half * sine_part],
        axis=-1,
    )


def encode_context(images, counts, qkv_enc):
    num_img = images.shape[0]
    num_patch = images.shape[1]
    head_dim = DV // HV
    local_heads = qkv_enc.shape[2] // head_dim
    normalized_rows = layer_norm(images.astype(jnp.float32)).astype(jnp.bfloat16)
    projected_rows = jnp.einsum(
        "ipd,jdc->jipc", normalized_rows, qkv_enc, preferred_element_type=jnp.float32
    ).astype(jnp.bfloat16)
    queries = projected_rows[0].reshape(num_img, num_patch, local_heads, head_dim)
    key_rows = projected_rows[1].reshape(num_img, num_patch, local_heads, head_dim)
    value_rows = projected_rows[2].reshape(num_img, num_patch, local_heads, head_dim)
    scores = jnp.einsum(
        "iphd,ikhd->ihpk", queries, key_rows, preferred_element_type=jnp.float32
    ) / math.sqrt(head_dim)
    valid = jnp.arange(num_patch, dtype=jnp.int32)[None, :] < 4 * counts[:, None]
    scores = jnp.where(valid[:, None, None, :], scores, -1e30)
    attn_probs = softmax_rows(scores).astype(jnp.bfloat16)
    context = jnp.einsum(
        "ihpk,ikhd->iphd", attn_probs, value_rows, preferred_element_type=jnp.float32
    ).astype(jnp.bfloat16)
    return context.reshape(num_img * num_patch, local_heads * head_dim)


def slot_layout(
    shard_id, per_dest, vis_count, image_session, session_slot, session_len, session_tenant
):
    num_images = vis_count.shape[0]
    num_sessions = session_slot.shape[0]
    image_idx = jnp.arange(num_images, dtype=jnp.int32)
    session_idx = jnp.arange(num_sessions, dtype=jnp.int32)
    same_session = image_session[:, None] == image_session[None, :]
    earlier = image_idx[None, :] < image_idx[:, None]
    offset = jnp.sum(jnp.where(same_session & earlier, vis_count[None, :], 0), axis=1)
    owner_match = image_session[None, :] == session_idx[:, None]
    image_slot = jnp.sum(jnp.where(owner_match, session_slot[:, None], 0), axis=0)
    dest_all = image_slot // SESS_DEV
    encoder_of = image_idx // IMG_DEV
    same_route = (
        (encoder_of[None, :] == encoder_of[:, None])
        & (dest_all[None, :] == dest_all[:, None])
        & earlier
    )
    rank_all = jnp.sum(same_route.astype(jnp.int32), axis=1)
    image_base = (encoder_of * per_dest + rank_all) * VMAX
    row_ids = jnp.arange(TOK_DEV, dtype=jnp.int32)
    position = row_ids % SLOT
    row_slot = shard_id * SESS_DEV + row_ids // SLOT
    slot_match = session_slot[None, :] == row_slot[:, None]
    row_len = jnp.sum(jnp.where(slot_match, session_len[None, :], 0), axis=1)
    tenant_of_row = jnp.sum(jnp.where(slot_match, session_tenant[None, :], 0), axis=1)
    member = (
        (image_slot[None, :] == row_slot[:, None])
        & (offset[None, :] <= position[:, None])
        & (position[:, None] < offset[None, :] + vis_count[None, :])
    )
    source = jnp.sum(
        jnp.where(member, image_base[None, :] + position[:, None] - offset[None, :], 0), axis=1
    )
    is_visual = jnp.any(member, axis=1)
    return (dest_all, rank_all, position, row_len, tenant_of_row, is_visual, source)


def decode_rows(
    tokens,
    sum_squares,
    down_projection_sums,
    flattened_qkv_weight,
    flattened_up_weight,
    position,
    row_len,
    tenant_of_row,
):
    num_rows = tokens.shape[0]
    root_mean_square = jnp.sqrt(sum_squares / DECODER_WIDTH + EPSILON)
    normalized_rows = (tokens.astype(jnp.float32) / root_mean_square[:, None]).astype(jnp.bfloat16)
    adapter_column_view = jnp.arange(down_projection_sums.shape[1], dtype=jnp.int32) // ADAPTER_RANK
    adapter_input_rows = jnp.where(
        adapter_column_view[None, :] == tenant_of_row[:, None],
        down_projection_sums / root_mean_square[:, None],
        0.0,
    ).astype(jnp.bfloat16)
    projected_rows = jnp.dot(
        normalized_rows, flattened_qkv_weight, preferred_element_type=jnp.float32
    ) + jnp.dot(adapter_input_rows, flattened_up_weight, preferred_element_type=jnp.float32)
    groups = projected_rows.shape[1] // ((QUERY_PER_KEY + 2) * DECODER_HEAD_DIM)
    projected_rows = projected_rows.reshape(num_rows, groups, QUERY_PER_KEY + 2, DECODER_HEAD_DIM)
    pos_float = position.astype(jnp.float32)
    queries = rotate(projected_rows[:, :, :QUERY_PER_KEY], pos_float).astype(jnp.bfloat16)
    key_rows = rotate(projected_rows[:, :, QUERY_PER_KEY], pos_float).astype(jnp.bfloat16)
    value_rows = projected_rows[:, :, QUERY_PER_KEY + 1].astype(jnp.bfloat16)
    queries = queries.reshape(SESS_DEV, SLOT, groups, QUERY_PER_KEY, DECODER_HEAD_DIM)
    key_rows = key_rows.reshape(SESS_DEV, SLOT, groups, DECODER_HEAD_DIM)
    value_rows = value_rows.reshape(SESS_DEV, SLOT, groups, DECODER_HEAD_DIM)
    scores = jnp.einsum(
        "sqgjd,skgd->sgjqk", queries, key_rows, preferred_element_type=jnp.float32
    ) / math.sqrt(DECODER_HEAD_DIM)
    slot_pos = jnp.arange(SLOT, dtype=jnp.int32)
    causal = slot_pos[None, :] <= slot_pos[:, None]
    scores = jnp.where(causal, scores, -1e30)
    attn_probs = softmax_rows(scores).astype(jnp.bfloat16)
    result = jnp.einsum(
        "sgjqk,skgd->sqgjd", attn_probs, value_rows, preferred_element_type=jnp.float32
    )
    result = result.reshape(num_rows, groups * QUERY_PER_KEY * DECODER_HEAD_DIM)
    return jnp.where((position < row_len)[:, None], result, 0.0)


def on_device(
    patches,
    vit_qkv,
    vit_out,
    merge_weight,
    query_key_value_weight,
    adapter_down,
    adapter_up_weight,
    text_embed,
    vis_count,
    image_session,
    session_slot,
    session_tenant,
    session_len,
):
    num_seq = lax.axis_size("seq")
    shard_id = lax.axis_index("seq")
    per_dest = IMG_DEV // num_seq
    num_img = patches.shape[0]
    num_patch = patches.shape[1]
    qkv_enc, out_enc = (
        lax.all_gather(vit_qkv, "seq", axis=1, tiled=True),
        lax.all_gather(vit_out, "seq", axis=1, tiled=True),
    )
    counts_here = lax.dynamic_slice_in_dim(vis_count, shard_id * IMG_DEV, IMG_DEV)
    context = encode_context(patches, counts_here, qkv_enc)
    flat_patch = patches.reshape(num_img * num_patch, DV)
    share_rows = context.shape[0] // lax.axis_size("tp")
    summed_share = lax.psum_scatter(
        jnp.dot(context, out_enc, preferred_element_type=jnp.float32),
        "tp",
        scatter_dimension=0,
        tiled=True,
    )
    own_patch = lax.dynamic_slice_in_dim(
        flat_patch, lax.axis_index("tp") * share_rows, share_rows, 0
    )
    share_in = (
        layer_norm(own_patch.astype(jnp.float32) + summed_share)
        .reshape(share_rows // 4, 4 * DV)
        .astype(jnp.bfloat16)
    )
    merged = jnp.dot(
        lax.all_gather(share_in, "tp", axis=0, tiled=True),
        merge_weight,
        preferred_element_type=jnp.float32,
    ).astype(jnp.bfloat16)
    merged = merged.reshape(num_img, VMAX, merged.shape[1])
    dest_all, rank_all, position, row_len, tenant_of_row, is_visual, source = slot_layout(
        shard_id, per_dest, vis_count, image_session, session_slot, session_len, session_tenant
    )
    here_dest = lax.dynamic_slice_in_dim(dest_all, shard_id * IMG_DEV, IMG_DEV)
    here_rank = lax.dynamic_slice_in_dim(rank_all, shard_id * IMG_DEV, IMG_DEV)
    dest_match = jnp.arange(num_seq, dtype=jnp.int32)[:, None, None] == here_dest[None, None, :]
    rank_match = jnp.arange(per_dest, dtype=jnp.int32)[None, :, None] == here_rank[None, None, :]
    pick_dest = (dest_match & rank_match).astype(jnp.bfloat16)
    outgoing = jnp.einsum(
        "rji,imc->rjmc", pick_dest, merged, preferred_element_type=jnp.float32
    ).astype(jnp.bfloat16)
    outgoing = outgoing.reshape(num_seq, per_dest * VMAX, merged.shape[2])
    incoming = lax.all_to_all(outgoing, "seq", split_axis=0, concat_axis=0, tiled=True)
    flat_rows = incoming.reshape(num_seq * per_dest * VMAX, incoming.shape[2])
    visual_rows = jnp.take(flat_rows, source, axis=0)
    tokens_part = jnp.where(
        is_visual[:, None],
        visual_rows,
        jnp.where((position < row_len)[:, None], text_embed, jnp.zeros_like(text_embed)),
    )
    raw_part = tokens_part.astype(jnp.float32)
    sum_squares, down_projection_sums = lax.psum(
        (
            jnp.sum(raw_part * raw_part, axis=1),
            jnp.dot(tokens_part, adapter_down, preferred_element_type=jnp.float32),
        ),
        "tp",
    )
    tokens = lax.all_gather(tokens_part, "tp", axis=1, tiled=True)
    dec_weight = lax.all_gather(query_key_value_weight, "seq", axis=0, tiled=True)
    flattened_qkv_weight = dec_weight.reshape(
        DECODER_WIDTH, dec_weight.shape[1] * (QUERY_PER_KEY + 2) * DECODER_HEAD_DIM
    )
    flattened_up_weight = adapter_up_weight.reshape(
        adapter_up_weight.shape[0],
        adapter_up_weight.shape[1] * (QUERY_PER_KEY + 2) * DECODER_HEAD_DIM,
    )
    return decode_rows(
        tokens,
        sum_squares,
        down_projection_sums,
        flattened_qkv_weight,
        flattened_up_weight,
        position,
        row_len,
        tenant_of_row,
    )


def solution(mesh):
    placed = (
        P("seq", None, None),
        P(None, "seq", "tp"),
        P("tp", "seq"),
        P(None, "tp"),
        P("seq", "tp", None, None),
        P("tp", None),
        P(None, "tp", None, None),
        P("seq", "tp"),
        P(),
        P(),
        P(),
        P(),
        P(),
    )
    return jax.shard_map(
        on_device, mesh=mesh, in_specs=placed, out_specs=P("seq", "tp"), check_vma=False
    )
```

profile of v0, /device:TPU:1, one launch (start us, length us, event | category | flops | bytes accessed | tf_op | source)
XLA Modules:
  0.0 428.9 jit_solution(13455384981636808815)
XLA Ops:
  6.5 0.7 all-gather.5.cloned.1.call-update
  7.3 26.6 %all_gather.16 = bf16[160,1280]{0,1:T(8,128)(2,1)S(1)} all-gather(bf16[160,40]{0,1:T(8,128)(2,1)} %param.15), channel_id=1, replica_groups=mesh['seq'=32,'tp'=8] {'seq'}, dimensions={1}, use_global_device_ids=true | all-gather | bytes 422400 | tf_op jit(solution)/shard_map/all_gather | solution.py:185
  33.9 0.8 dynamic-slice_multiply_fusion
  34.6 1.6 convert_reduce_fusion.1
  36.2 0.5 fusion.8
  36.8 26.3 %all-gather.5.cloned.1.call-done = bf16[3,1280,160]{2,1,0:T(8,128)(2,1)} async-done(((bf16[3,40,160]{2,1,0:T(8,128)(2,1)}), bf16[3,1280,160]{2,1,0:T(8,128)(2,1)}) %all-gather.5.cloned.1.call-update) | async-done | bytes 1228816 | tf_op jit(solution)/shard_map/all_gather | solution.py:184
  63.1 2.8 fusion.20
  66.4 0.3 fusion.28
  66.7 0.8 copy-done.11
  67.5 0.2 fusion.78
  67.7 1.7 fusion.29
  69.8 2.1 fusion.80
  72.0 39.1 %reduce-scatter.2.cloned.1.call-done = f32[64,1280]{1,0:T(8,128)} async-done(((f32[512,1280]{1,0:T(8,128)}), f32[64,1280]{1,0:T(8,128)}) %reduce-scatter.2.cloned.1.call-update) | async-done | bytes 327696 | tf_op jit(solution)/shard_map/reduce_scatter | solution.py:191
  111.1 1.1 fusion.45
  112.2 1.2 multiply_reduce_fusion.1
  113.4 1.1 multiply_convert_fusion
  114.5 0.8 convert_element_type.105
  115.5 0.7 select_reduce_fusion
  116.2 1.6 convert_reduce_fusion
  118.0 0.5 fusion.59
  118.6 0.5 select_reduce_fusion.1
  119.1 35.0 %all-gather.7.cloned.1.call-done = bf16[128,5120]{1,0:T(8,128)(2,1)} async-done(((bf16[16,5120]{1,0:T(8,128)(2,1)}), bf16[128,5120]{1,0:T(8,128)(2,1)}) %all-gather.7.cloned.1.call-update) | async-done | bytes 1310736 | tf_op jit(solution)/shard_map/all_gather | solution.py:206
  154.0 5.9 %convolution_convert_fusion.2 = bf16[128,1024]{1,0:T(8,128)(2,1)S(1)} fusion(bf16[128,5120]{1,0:T(8,128)(2,1)} %all-gather.7.cloned.1.call-done, bf16[5120,1024]{1,0:T(8,128)(2,1)} %param.16), kind=kOutput, calls=%fused_computation.34 | convolution fusion | flops 1342308352 | bytes 12058624 | tf_op jit(solution)/shard_map/dot_general | solution.py:205
  160.1 0.2 convolution_convert_fusion
  160.3 0.9 copy.62
  161.2 11.7 %all-to-all-start = ((bf16[32,4,1024]{2,1,0:T(4,128)(2,1)}), bf16[32,4,1024]{2,1,0:T(4,128)(2,1)S(1)}, u32[]{:S(2)}, u32[]{:S(2)}) async-start(bf16[32,4,1024]{2,1,0:T(4,128)(2,1)} %copy.62), calls=%async_computation.1 | async-start | bytes 524288 | tf_op jit(solution)/shard_map/all_to_all | solution.py:223
  172.9 0.2 all-reduce.2.cloned.1.call-start
  173.2 8.6 %all-to-all-done = bf16[32,4,1024]{2,1,0:T(4,128)(2,1)S(1)} async-done(((bf16[32,4,1024]{2,1,0:T(4,128)(2,1)}), bf16[32,4,1024]{2,1,0:T(4,128)(2,1)S(1)}, u32[]{:S(2)}, u32[]{:S(2)}) %all-to-all-start) | async-done | bytes 262176 | tf_op jit(solution)/shard_map/all_to_all | solution.py:223
  181.9 1.2 gather_fusion
  183.1 0.4 multiply_reduce_fusion
  183.5 0.9 fusion.81
  184.5 0.5 all-gather.9.cloned.1.call-update
  185.1 1.1 copy.63
  186.5 0.3 multiply_cosine_fusion
  186.8 12.5 %psum.14 = f32[256]{0:T(256)S(1)} all-reduce(f32[256]{0:T(256)S(1)} %get-tuple-element.7), channel_id=1, replica_groups=mesh['seq'=32,'tp'=8] {'tp'}, use_global_device_ids=true, to_apply=%region_14.15 | all-reduce | flops 256 | bytes 2048 | tf_op jit(solution)/shard_map/psum | solution.py:232
  199.3 47.0 %all-reduce.2.cloned.1.call-done = f32[256,128]{1,0:T(8,128)} async-done(((f32[256,128]{1,0:T(8,128)}), f32[256,128]{1,0:T(8,128)}) %all-reduce.2.cloned.1.call-update) | async-done | bytes 131088 | tf_op jit(solution)/shard_map/psum | solution.py:232
  246.3 1.3 fusion.52
  247.6 58.8 %all-gather.9.cloned.1.call-done = bf16[256,8192]{1,0:T(8,128)(2,1)} async-done(((bf16[256,1024]{1,0:T(8,128)(2,1)}), bf16[256,8192]{1,0:T(8,128)(2,1)}) %all-gather.9.cloned.1.call-update) | async-done | bytes 4194320 | tf_op jit(solution)/shard_map/all_gather | solution.py:239
  306.4 98.8 %all-gather.11.cloned.1.call-done = bf16[8192,1,10,128]{0,3,2,1:T(8,128)(2,1)} async-done(((bf16[256,1,10,128]{0,3,2,1:T(8,128)(2,1)}), bf16[8192,1,10,128]{0,3,2,1:T(8,128)(2,1)}) %all-gather.11.cloned.1.call-update) | async-done | bytes 20971536 | tf_op jit(solution)/shard_map/all_gather | solution.py:240
  405.2 12.2 %fusion.7 = f32[256,1280]{1,0:T(8,128)S(1)} fusion(f32[256,1280]{1,0:T(8,128)S(1)} %fusion.52, bf16[8192,1280]{0,1:T(8,128)(2,1)} %bitcast.107, bf16[256,8192]{1,0:T(8,128)(2,1)} %all-gather.9.cloned.1.call-done, f32[256]{0:T(256)S(1)} %add_sqrt_fusion), kind=kOutput, calls=%fused_computation.14 | convolution fusion | flops 5375328256 | bytes 27788288 | tf_op jit(solution)/shard_map/dot_general | solution.py:137
  417.4 0.4 copy.65
  418.1 0.3 copy.70
  418.5 0.3 copy.69
  418.8 0.3 fusion.49
  419.4 0.5 fusion.79
  420.1 0.3 convolution_bitcast_fusion
  420.4 0.4 copy.73
  420.8 1.2 bitcast_select_fusion
  (73 shorter events, 3.0 us)
Async XLA Ops:
  6.5 177.0 %copy-start = (bf16[1024,128]{1,0:T(8,128)(2,1)S(1)}, bf16[1024,128]{1,0:T(8,128)(2,1)}, u32[]{:S(2)}) copy-start(bf16[1024,128]{1,0:T(8,128)(2,1)} %param.18) | copy-start | bytes 786436
  6.5 29.7 %copy-start.1 = (bf16[32,16,1280]{2,1,0:T(8,128)(2,1)S(1)}, bf16[32,16,1280]{2,1,0:T(8,128)(2,1)}, u32[]{:S(2)}) copy-start(bf16[32,16,1280]{2,1,0:T(8,128)(2,1)} %param.13) | copy-start | bytes 3932164
  6.5 56.5 %all-gather.5.cloned.1.call-start = ((), (), s32[]{:S(2)}) async-start(), calls=%async_computation.2 | async-start | bytes 2027520 | tf_op jit(solution)/shard_map/all_gather | solution.py:184
  7.3 103.8 %reduce-scatter.2.cloned.1.call-start = ((), (), s32[]{:S(2)}) async-start(), calls=%async_computation.3 | async-start | bytes 2949120 | tf_op jit(solution)/shard_map/reduce_scatter | solution.py:191
  66.7 0.8 copy-start.11
  71.9 43.4 %copy-start.7 = (s32[1024]{0:T(1024)S(1)}, s32[1024]{0:T(1024)}, u32[]{:S(2)}) copy-start(s32[1024]{0:T(1024)} %param.22) | copy-start | bytes 12292
  71.9 43.4 %copy-start.8 = (s32[64]{0:T(128)S(1)}, s32[64]{0:T(128)}, u32[]{:S(2)}) copy-start(s32[64]{0:T(128)} %param.23) | copy-start | bytes 772
  71.9 43.6 %copy-start.6 = (s32[1024]{0:T(1024)S(1)}, s32[1024]{0:T(1024)}, u32[]{:S(2)}) copy-start(s32[1024]{0:T(1024)} %param.21) | copy-start | bytes 12292
  71.9 46.0 %copy-start.9 = (s32[64]{0:T(128)S(1)}, s32[64]{0:T(128)}, u32[]{:S(2)}) copy-start(s32[64]{0:T(128)} %param.24) | copy-start | bytes 772
  71.9 46.0 %copy-start.10 = (s32[64]{0:T(128)S(1)}, s32[64]{0:T(128)}, u32[]{:S(2)}) copy-start(s32[64]{0:T(128)} %param.25) | copy-start | bytes 772
  71.9 82.1 %all-gather.7.cloned.1.call-start = ((), (), s32[]{:S(2)}) async-start(), calls=%async_computation.4 | async-start | bytes 1474560 | tf_op jit(solution)/shard_map/all_gather | solution.py:206
  161.2 20.6 %all-to-all-start = ((bf16[32,4,1024]{2,1,0:T(4,128)(2,1)}), bf16[32,4,1024]{2,1,0:T(4,128)(2,1)S(1)}, u32[]{:S(2)}, u32[]{:S(2)}) async-start(bf16[32,4,1024]{2,1,0:T(4,128)(2,1)} %copy.62), calls=%async_computation.1 | async-start | bytes 524288 | tf_op jit(solution)/shard_map/all_to_all | solution.py:223
  172.9 73.4 %all-reduce.2.cloned.1.call-start = ((), (), s32[]{:S(2)}) async-start(), calls=%async_computation.7 | async-start | bytes 262144 | tf_op jit(solution)/shard_map/psum | solution.py:232
  173.1 9.9 %copy-start.4 = (bf16[256,1024]{1,0:T(8,128)(2,1)S(1)}, bf16[256,1024]{1,0:T(8,128)(2,1)}, u32[]{:S(2)}) copy-start(bf16[256,1024]{1,0:T(8,128)(2,1)} %param.20) | copy-start | bytes 1572868
  183.0 2.1 copy-start.3
  183.0 3.2 copy-start.5
  183.5 1.0 copy-start.2
  184.5 121.9 %all-gather.9.cloned.1.call-start = ((), (), s32[]{:S(2)}) async-start(), calls=%async_computation.5 | async-start | bytes 4718592 | tf_op jit(solution)/shard_map/all_gather | solution.py:239
  185.1 220.1 %all-gather.11.cloned.1.call-start = ((), (), s32[]{:S(2)}) async-start(), calls=%async_computation.6 | async-start | bytes 21626880 | tf_op jit(solution)/shard_map/all_gather | solution.py:240
Sparse Core Ops, SparseCore 0:
  10.0 52.9 all-gather.4
  72.0 38.9 reduce-scatter.1
  115.4 38.5 all-gather.6
  184.6 61.6 all-reduce.1
  248.1 58.2 all-gather.8
  309.0 96.1 all-gather.10
where the time goes:
time: 429 us
  waiting for transfers between devices  315 us (73%)
  blocking collectives  39 us (9%)
  matrix products  28.2 us (7%)
  between operations  14 us (3%)
  other arithmetic  12.8 us (3%)
  starting transfers between devices  12.1 us (3%)
  local copies, waits for them, and re-layouts  8.05 us (2%)
    all_gather x1, waiting for transfers between devices, on_device(): lax.all_gather(query_key_value_weight, 'seq', axis=0, tiled=True)  98.8 us
    all_gather x1, waiting for transfers between devices, on_device(): tokens = lax.all_gather(tokens_part, 'tp', axis=1, tiled=True)  58.8 us
    psum x1, waiting for transfers between devices, on_device(): lax.psum((jnp.sum(raw_part * raw_part, axis=1), jnp.dot(tokens_part, adap...  47 us
    reduce_scatter x1, waiting for transfers between devices, on_device(): lax.psum_scatter(jnp.dot(context, out_enc, preferred_element_type=jnp.flo...  39.1 us
    all_gather x1, waiting for transfers between devices, on_device(): lax.all_gather(share_in, 'tp', axis=0, tiled=True)  35 us
    all_gather x1, blocking collectives, on_device(): lax.all_gather(vit_out, 'seq', axis=1, tiled=True)  26.6 us
    all_gather x1, waiting for transfers between devices, on_device(): lax.all_gather(vit_qkv, 'seq', axis=1, tiled=True)  26.3 us
    psum x1, blocking collectives, on_device(): lax.psum((jnp.sum(raw_part * raw_part, axis=1), jnp.dot(tokens_part, adap...  12.5 us
  transfers between devices with their start and end apart: 7, of which 7 were waited for; matrix products, arithmetic and copies ran while one was open for 2% of the time, Pallas kernels for 0%

commit v1 on v0

v1 whole, which is shorter than its diff:
```python
import functools
import math

import jax
import jax.numpy as jnp
import numpy as np
from jax import lax
from jax.experimental import pallas as pl
from jax.experimental.pallas import tpu as pltpu
from jax.sharding import PartitionSpec as P

DV = 1280
HV = 16
HEAD = 80
DECODER_WIDTH = 8192
DECODER_HEAD_DIM = 128
ADAPTER_RANK = 16
IMG_DEV = 32
VMAX = 4
SLOT = 128
QUERY_PER_KEY = 8
N_SEQ = 32
N_TP = 8
COLS = 1280
EPSILON = 1e-06
ROPE_BASE = 1000000.0
MESH = pl.DeviceIdType.MESH
F32 = jnp.float32
BF16 = jnp.bfloat16


def tables():
    perm = np.zeros((512, 512), np.float32)
    for j in range(4):
        for i in range(32):
            for m in range(4):
                perm[j * 128 + i * 4 + m, i * 16 + m * 4 + j] = 1
    select = np.zeros((640, 768), np.float32)
    for group in range(6):
        for lane in range(HEAD):
            select[group * HEAD + lane, group * 128 + lane] = 1
    select_out = np.zeros((160, 640), np.float32)
    for row in range(160):
        select_out[row, 480 + row] = 1
    half = DECODER_HEAD_DIM // 2
    inverse_freq = np.power(
        np.float32(ROPE_BASE), -(np.arange(half, dtype=np.float32) * 2.0 / DECODER_HEAD_DIM)
    ).astype(np.float32)
    angles = np.arange(SLOT, dtype=np.float32)[:, None] * inverse_freq[None, :]
    cosine = np.cos(angles).astype(np.float32)
    sine = np.sin(angles).astype(np.float32)
    return (
        jnp.asarray(perm, BF16),
        jnp.asarray(select, BF16),
        jnp.asarray(select_out, BF16),
        jnp.asarray(np.concatenate([cosine, cosine], 1)),
        jnp.asarray(np.concatenate([-sine, sine], 1)),
    )


def weight_copies():
    whole, first, second = (0, 256), (0, 128), (128, 128)

    def sib(blocks):
        return [(by, bx, 0, 256, 0, 0, True) for by, bx in blocks]

    def go(by, bx, part, ty, tx):
        return (by, bx, part[0], part[1], ty, tx, False)

    stage0 = [go(0, 0, whole, 0, 1), go(0, 0, whole, 0, -1), go(0, 0, whole, 1, 0), go(0, 0, whole, -1, 0)]
    stage0 += sib([(0, 0)])
    stage1 = [
        go(0, -1, first, 0, 1), go(0, 1, second, 0, -1), go(-1, 0, first, 1, 0), go(1, 0, second, -1, 0),
    ]
    for side in (-1, 1):
        for to in (-1, 1):
            stage1 += [go(0, side, first, to, 0), go(side, 0, second, 0, to)]
    stage1 += sib([(0, -1), (0, 1), (-1, 0), (1, 0)])
    stage2 = [
        go(0, 2, first, 1, 0), go(0, 2, first, -1, 0), go(2, 0, second, 0, 1), go(2, 0, second, 0, -1),
        go(-1, 1, first, 1, 0), go(1, -1, first, -1, 0), go(1, -1, second, 0, 1), go(-1, 1, second, 0, -1),
    ]
    stage2 += sib([(0, 2), (2, 0), (-1, -1), (-1, 1), (1, -1), (1, 1)])
    stage3 = [
        go(-1, 2, (0, 64), 1, 0), go(1, 2, (64, 64), -1, 0), go(2, -1, (128, 64), 0, 1), go(2, 1, (192, 64), 0, -1),
    ]
    stage3 += sib([(-1, 2), (1, 2), (2, -1), (2, 1)])
    stage4 = sib([(2, 2)])
    stages, count = [], 0
    for stage in (stage0, stage1, stage2, stage3, stage4):
        stages.append([(count + i,) + entry for i, entry in enumerate(stage)])
        count += len(stage)
    return stages, count


STAGES, W_COPIES = weight_copies()


def bdot(a, b):
    return jnp.dot(a, b, preferred_element_type=F32)


def bdot_nt(a, b):
    return lax.dot_general(a, b, (((1,), (1,)), ((), ())), preferred_element_type=F32)


def normalize(values):
    mean_val = jnp.mean(values, axis=-1, keepdims=True)
    centered = values - mean_val
    variance = jnp.mean(centered * centered, axis=-1, keepdims=True)
    return centered * lax.rsqrt(variance + EPSILON)


def kernel(
    patches, vit, mw, w, down, up, text, tgt, key, bias, tmask, keep, tenant_mask,
    perm, select, select_out, cosine, sine,
    out,
    g, wf, wall, pp, ln, qkv, o_all, ctx_all, enc, mwb, vis, xs, ys, tok, dl, w_all, acc,
    loc_sem, mw_sem, gs_sem, gr_sem, fs_sem, fr_sem, ws_sem, wr_sem,
    os_sem, or_sem, ofs_sem, ofr_sem, cs_sem, cr_sem, es_sem, er_sem, ls_sem, lr_sem,
    as_sem, ar_sem, ds_sem, dr_sem,
):
    s = lax.axis_index("seq")
    t = lax.axis_index("tp")
    core = lax.rem(s, 2)
    chip = s // 2
    cx = lax.rem(chip, 4)
    cy = chip // 4
    sibling = s + 1 - 2 * core

    def chip_at(dy, dx):
        return lax.rem(cy + (dy + 4), 4) * 4 + lax.rem(cx + (dx + 4), 4)

    def rows(ref, start, size, step=16):
        return ref.at[pl.ds(pl.multiple_of(start, step), size)]

    def arrived(ref, sem):
        pltpu.make_async_copy(ref, ref, sem).wait()

    barrier = pltpu.get_barrier_semaphore()

    def greet_seq(i, carry):
        pl.semaphore_signal(barrier, inc=1, device_id=(lax.rem(s + i, N_SEQ), t), device_id_type=MESH)
        return carry

    def greet_tp(i, carry):
        pl.semaphore_signal(barrier, inc=1, device_id=(s, lax.rem(t + i, N_TP)), device_id_type=MESH)
        return carry

    lax.fori_loop(1, N_SEQ, greet_seq, 0)
    lax.fori_loop(1, N_TP, greet_tp, 0)
    pl.semaphore_wait(barrier, N_SEQ + N_TP - 2)

    def g_row(c, chip_id):
        return (c * 16 + chip_id) * 48

    own_g = pltpu.make_async_copy(vit, rows(g, g_row(core, chip), 48), loc_sem.at[0])
    own_g.start()
    for dy in range(4):
        for dx in range(4):
            if dy == 0 and dx == 0:
                continue
            pltpu.make_async_remote_copy(
                src_ref=vit,
                dst_ref=rows(g, g_row(core, chip), 48),
                send_sem=gs_sem.at[0],
                recv_sem=gr_sem.at[(4 - dy) % 4],
                device_id=(chip_at(dy, dx) * 2 + core, t),
                device_id_type=MESH,
            ).start()

    own_w = pltpu.make_async_copy(w, rows(w_all, s * 256, 256), loc_sem.at[1])
    own_w.start()
    mw_loads = [
        pltpu.make_async_copy(mw.at[pl.ds(1280 * j, 1280)], mwb.at[j % 2], mw_sem.at[j]) for j in range(4)
    ]
    mw_loads[0].start()
    mw_loads[1].start()

    def w_ref(by, bx, first, size):
        return rows(w_all, (chip_at(by, bx) * 2 + core) * 256 + first, size)

    def w_start(stage):
        for index, by, bx, first, size, ty, tx, sib in STAGES[stage]:
            source = w if stage == 0 else w_ref(by, bx, first, size)
            pltpu.make_async_remote_copy(
                src_ref=source,
                dst_ref=w_ref(by, bx, first, size),
                send_sem=ws_sem.at[index],
                recv_sem=wr_sem.at[index],
                device_id=(sibling if sib else chip_at(ty, tx) * 2 + core, t),
                device_id_type=MESH,
            ).start()

    def w_arrived(stage):
        for index, by, bx, first, size, ty, tx, sib in STAGES[stage]:
            if not sib:
                arrived(w_ref(by - ty, bx - tx, first, size), wr_sem.at[index])

    def w_rest():
        for stage in STAGES:
            for index, by, bx, first, size, ty, tx, sib in stage:
                if sib:
                    arrived(rows(w_all, (chip_at(by, bx) * 2 + 1 - core) * 256, 256), wr_sem.at[index])

    def w_sent():
        for stage in STAGES:
            for index, by, bx, first, size, ty, tx, sib in stage:
                arrived(w_ref(by, bx, first, size), ws_sem.at[index])

    right = (s, lax.rem(t + 1, N_TP))
    left = (s, lax.rem(t + N_TP - 1, N_TP))

    def ring(buf, base, size, cut, send, recv):
        def part(way, origin, k):
            first = base(lax.rem(origin + 2 * N_TP, N_TP))
            if k < 3:
                return rows(buf, first, size)
            if way == 0:
                return rows(buf, first, cut)
            return rows(buf, first + cut, size - cut)

        def start(k):
            for way, to, origin in ((0, right, t - k), (1, left, t + k)):
                piece = part(way, origin, k)
                pltpu.make_async_remote_copy(
                    src_ref=piece, dst_ref=piece, send_sem=send.at[way * 4 + k], recv_sem=recv.at[way * 4 + k],
                    device_id=to, device_id_type=MESH,
                ).start()

        def wait(k):
            arrived(part(0, t - 1 - k, k), recv.at[k])
            arrived(part(1, t + 1 + k, k), recv.at[4 + k])

        def sent():
            for k in range(4):
                arrived(part(0, t - k, k), send.at[k])
                arrived(part(1, t + k, k), send.at[4 + k])

        return start, wait, sent

    e_start, e_wait, e_sent = ring(tok, lambda z: z * 256 + 128, 128, 64, es_sem, er_sem)
    l_start, l_wait, l_sent = ring(tok, lambda z: z * 256, 128, 64, ls_sem, lr_sem)
    o_start, o_wait, o_sent = ring(o_all, lambda z: z * 160 + 80 * core, 80, 48, os_sem, or_sem)
    c_start, c_wait, c_sent = ring(ctx_all, lambda z: z * 160, 160, 80, cs_sem, cr_sem)

    def o_share(k):
        origins = [(0, t - 1 - k), (1, t + 1 + k)] if k < 3 else [(0, t + 4)]
        for way, origin in origins:
            first = lax.rem(origin + 2 * N_TP, N_TP) * 160 + 80 * core
            piece = rows(o_all, first, 80)
            pltpu.make_async_remote_copy(
                src_ref=piece, dst_ref=piece, send_sem=ofs_sem.at[way * 4 + k], recv_sem=ofr_sem.at[way * 4 + k],
                device_id=(sibling, t), device_id_type=MESH,
            ).start()

    def o_shared(sems, c):
        for k in range(4):
            origins = [(0, t - 1 - k), (1, t + 1 + k)] if k < 3 else [(0, t + 4)]
            for way, origin in origins:
                first = lax.rem(origin + 2 * N_TP, N_TP) * 160 + 80 * c
                arrived(rows(o_all, first, 80), sems.at[way * 4 + k])

    own_tok = pl.multiple_of(t * 256, 256)
    for l in range(2):
        tok[pl.ds(own_tok + 128 + 64 * l, 64), :] = jnp.where(
            tmask[128 + 64 * l:192 + 64 * l, :] > 0, text[128 * l + 64:128 * l + 128, :], jnp.zeros((64, 1024), BF16)
        )
    e_start(0)

    for n in range(5):
        lanes = slice(256 * n, 256 * n + 256)
        pp[:, lanes] = bdot(perm[...], patches[:, lanes]).astype(BF16)
    for r in range(4):
        part = slice(128 * r, 128 * r + 128)
        ln[part, :] = normalize(pp[part, :].astype(F32)).astype(BF16)

    own_g.wait()
    arrived(g.at[pl.ds(0, 144)], gr_sem.at[0])
    for d in range(4):
        group = rows(g, g_row(core, lax.rem(cy + d, 4) * 4), 192)
        if d > 0:
            arrived(group, gr_sem.at[d])
        pltpu.make_async_remote_copy(
            src_ref=group, dst_ref=group, send_sem=fs_sem.at[d], recv_sem=fr_sem.at[d],
            device_id=(sibling, t), device_id_type=MESH,
        ).start()
    own_w.wait()
    w_start(0)
    for d in range(4):
        arrived(rows(g, g_row(1 - core, lax.rem(cy + d, 4) * 4), 192), fr_sem.at[d])
    e_wait(0)
    e_start(1)

    for b in range(32):
        first = g_row(b % 2, b // 2)
        wf[40 * b:40 * b + 40, :] = g[first:first + 48, :].astype(F32)[:40, :]
    for r in range(5):
        part = slice(256 * r, 256 * r + 256)
        wall[part, :] = wf[part, :].astype(BF16)
    own_o = pl.multiple_of(t * 160, 32)
    for r in range(5):
        part = slice(256 * r, 256 * r + 256)
        o_all[pl.ds(own_o, 160), part] = bdot_nt(select_out[...], wall[part, :]).astype(BF16)
    o_start(0)

    for n in range(5):
        lanes = slice(128 * n, 128 * n + 128)
        qkv[:, lanes] = bdot(ln[...], wall[:, lanes]).astype(BF16)
    scale = 1.0 / math.sqrt(HEAD)
    for h in range(2):
        q_h = bdot(qkv[...], select[:, 128 * h:128 * h + 128]).astype(BF16)
        k_h = bdot(qkv[...], select[:, 256 + 128 * h:384 + 128 * h]).astype(BF16)
        v_h = bdot(qkv[...], select[:, 512 + 128 * h:640 + 128 * h])
        v_t = jnp.transpose(v_h).astype(BF16)
        for q in range(4):
            scores = bdot_nt(k_h, q_h[128 * q:128 * q + 128, :]) * scale
            scores = scores.reshape(4, 128, 128) + bias[...][None]
            largest = jnp.max(jnp.max(scores, axis=0), axis=0, keepdims=True)
            exponent = jnp.exp(scores - largest[None])
            total = jnp.sum(jnp.sum(exponent, axis=0), axis=0, keepdims=True)
            probs = (exponent / total[None]).astype(BF16).reshape(512, 128)
            ctx_t = bdot(v_t, probs).astype(BF16)
            ctx_all[pl.ds(own_o + 80 * h, 80), 128 * q:128 * q + 128] = ctx_t[:80, :]
    c_start(0)

    o_wait(0)
    o_start(1)
    o_share(0)
    c_wait(0)
    c_start(1)
    w_arrived(0)
    w_start(1)
    o_wait(1)
    o_start(2)
    o_share(1)
    c_wait(1)
    c_start(2)
    o_wait(2)
    o_start(3)
    o_share(2)
    c_wait(2)
    c_start(3)
    e_wait(1)
    e_start(2)
    o_wait(3)
    o_share(3)
    c_wait(3)
    o_shared(ofr_sem, 1 - core)

    for r in range(4):
        part = slice(128 * r, 128 * r + 128)
        ln[part, :] = jnp.transpose(ctx_all[:, part].astype(F32)).astype(BF16)
    for n in range(5):
        lanes = slice(256 * n, 256 * n + 256)
        enc[:, lanes] = pp[:, lanes].astype(F32) + bdot(ln[...], o_all[:, lanes])
    for j in range(4):
        part = slice(128 * j, 128 * j + 128)
        merged_in = normalize(enc[part, :]).astype(BF16)
        mw_loads[j].wait()
        if j == 0:
            vis[...] = bdot(merged_in, mwb[j % 2])
        else:
            vis[...] += bdot(merged_in, mwb[j % 2])
        if j < 2:
            mw_loads[j + 2].start()

    row_512 = lax.broadcasted_iota(jnp.int32, (512, 128), 0)
    outgoing = jnp.zeros((512, 256), F32)
    for q in range(4):
        place = (row_512 == tgt[q:q + 1, :]).astype(F32).astype(BF16)
        outgoing += bdot(place, vis[:, 256 * q:256 * q + 256].astype(BF16))
    xs[...] = outgoing.astype(BF16)

    def send_rows(i, carry):
        to = lax.rem(s + i, N_SEQ)
        pltpu.make_async_remote_copy(
            src_ref=rows(xs, to * 16, 16), dst_ref=rows(ys, s * 16, 16),
            send_sem=as_sem.at[0], recv_sem=ar_sem.at[0], device_id=(to, t), device_id_type=MESH,
        ).start()
        return carry

    lax.fori_loop(1, N_SEQ, send_rows, 0)
    own_y = pl.ds(pl.multiple_of(s * 16, 16), 16)
    ys[own_y, :] = xs[own_y, :]
    w_arrived(1)
    w_start(2)
    e_wait(2)
    e_start(3)
    arrived(ys.at[pl.ds(0, 496)], ar_sem.at[0])

    row_128 = lax.broadcasted_iota(jnp.int32, (128, 512), 0)
    for q in range(4):
        lanes = slice(256 * q, 256 * q + 256)
        place = (row_128 == key[q:q + 1, :]).astype(F32).astype(BF16)
        picked = bdot(place, ys[...]).astype(BF16)
        for l in range(2):
            half = slice(64 * l, 64 * l + 64)
            tok[pl.ds(own_tok + 64 * l, 64), lanes] = jnp.where(
                tmask[half, :] > 0, text[128 * l:128 * l + 64, lanes], picked[half, :]
            )
    l_start(0)

    down_sums = jnp.transpose(bdot(tok[pl.ds(own_tok, 256), :], down[...])) * tenant_mask[...]
    dl[pl.ds(pl.multiple_of(t * 16, 16), 16), :] = jnp.sum(down_sums.reshape(8, 16, 256), axis=0)

    def send_down(i, carry):
        piece = rows(dl, t * 16, 16)
        pltpu.make_async_remote_copy(
            src_ref=piece, dst_ref=piece, send_sem=ds_sem.at[0], recv_sem=dr_sem.at[0],
            device_id=(s, lax.rem(t + i, N_TP)), device_id_type=MESH,
        ).start()
        return carry

    lax.fori_loop(1, N_TP, send_down, 0)

    w_arrived(2)
    w_start(3)
    l_wait(0)
    l_start(1)
    e_wait(3)
    w_arrived(3)
    w_start(4)
    l_wait(1)
    l_start(2)
    w_rest()

    def project(z):
        x = tok[pl.ds(pl.multiple_of(z * 256, 256), 256), :]
        first = pl.multiple_of(z * 1024, 1024)
        for n in range(5):
            lanes = slice(256 * n, 256 * n + 256)
            acc[:, lanes] += bdot(x, w_all[pl.ds(first, 1024), lanes])
        x_wide = x.astype(F32)
        return jnp.sum(x_wide * x_wide, axis=1, keepdims=True)

    acc[...] = jnp.zeros_like(acc)
    squares = project(t)
    squares += project(lax.rem(t + 1, N_TP))
    squares += project(lax.rem(t + 7, N_TP))
    l_wait(2)
    l_start(3)
    for k in (2, 6, 3, 5):
        squares += project(lax.rem(t + k, N_TP))
    arrived(dl.at[pl.ds(0, 112)], dr_sem.at[0])
    down_t = jnp.sum(dl[...].reshape(8, 16, 256), axis=0)
    lora = jnp.transpose(jnp.concatenate([down_t] * 8, axis=0) * tenant_mask[...]).astype(BF16)
    acc[...] += bdot(lora, up[...])
    l_wait(3)
    squares += project(lax.rem(t + 4, N_TP))
    inverse = lax.rsqrt(squares * (1.0 / DECODER_WIDTH) + EPSILON)

    causal = lax.broadcasted_iota(jnp.int32, (128, 128), 0) >= lax.broadcasted_iota(jnp.int32, (128, 128), 1)
    for l in range(2):
        low, high = slice(64 * l, 64 * l + 64), slice(128 + 64 * l, 192 + 64 * l)
        factor = jnp.concatenate([inverse[low, :], inverse[high, :]], axis=0)

        def column(index):
            lanes = slice(128 * index, 128 * index + 128)
            return jnp.concatenate([acc[low, lanes], acc[high, lanes]], axis=0) * factor

        def rotate(values):
            return values * cosine[...] + pltpu.roll(values, 64, 1) * sine[...]

        key_rows = rotate(column(8)).astype(BF16)
        value_rows = column(9).astype(BF16)
        kept = keep[128 * l:128 * l + 128, :] > 0
        for j in range(QUERY_PER_KEY):
            query = rotate(column(j)).astype(BF16)
            scores = bdot_nt(query, key_rows) * (1.0 / math.sqrt(DECODER_HEAD_DIM))
            scores = jnp.where(causal, scores, -1e30)
            exponent = jnp.exp(scores - jnp.max(scores, axis=1, keepdims=True))
            probs = (exponent / jnp.sum(exponent, axis=1, keepdims=True)).astype(BF16)
            out[128 * l:128 * l + 128, 128 * j:128 * j + 128] = jnp.where(kept, bdot(probs, value_rows), 0.0)

    arrived(g.at[pl.ds(0, 720)], gs_sem.at[0])
    for d in range(4):
        arrived(rows(g, g_row(core, lax.rem(cy + d, 4) * 4), 192), fs_sem.at[d])
    w_sent()
    e_sent()
    l_sent()
    o_sent()
    c_sent()
    o_shared(ofs_sem, core)
    arrived(xs.at[pl.ds(0, 496)], as_sem.at[0])
    arrived(dl.at[pl.ds(0, 112)], ds_sem.at[0])


def layout(shard_id, vis_count, image_session, session_slot, session_len, session_tenant):
    owner = image_session[None, :] == jnp.arange(session_slot.shape[0], dtype=jnp.int32)[:, None]
    image_slot = jnp.sum(jnp.where(owner, session_slot[:, None], 0), axis=0).reshape(N_SEQ, IMG_DEV)
    counts = vis_count.reshape(N_SEQ, IMG_DEV)
    here_dest = lax.dynamic_slice_in_dim(image_slot, shard_id, 1, 0)[0] // 2
    here_count = lax.dynamic_slice_in_dim(counts, shard_id, 1, 0)[0]
    quarter = jnp.arange(8, dtype=jnp.int32)
    merged = jnp.arange(128, dtype=jnp.int32)
    tgt = jnp.repeat(here_dest, VMAX)[None, :] * 16 + quarter[:, None] * 4 + (merged % 4)[None, :]
    same_image = (merged[:, None] // 4 == merged[None, :] // 4) & (
        (merged % 4) < jnp.repeat(here_count, VMAX)
    )[:, None]
    bias = jnp.where(same_image, 0.0, -1e30).astype(F32)
    mine = image_slot // 2 == shard_id
    count = jnp.sum(jnp.where(mine, counts, 0), axis=1)
    place = jnp.sum(jnp.where(mine, image_slot % 2, 0), axis=1)
    encoder = jnp.arange(N_SEQ, dtype=jnp.int32)
    before = (place[:, None] == place[None, :]) & (encoder[None, :] < encoder[:, None])
    offset = jnp.sum(jnp.where(before, count[None, :], 0), axis=1)
    column = jnp.arange(512, dtype=jnp.int32)
    valid = ((column // 4) % 4)[None, :] == quarter[:, None]
    valid = valid & (column % 4 < jnp.repeat(count, 16))[None, :]
    key = jnp.where(valid, (jnp.repeat(place * 64 + offset, 16) + column % 4)[None, :], -1)
    two = jnp.arange(2, dtype=jnp.int32)
    total = jnp.sum(jnp.where(place[None, :] == two[:, None], count[None, :], 0), axis=1)
    match = session_slot[None, :] == (shard_id * 2 + two)[:, None]
    length = jnp.sum(jnp.where(match, session_len[None, :], 0), axis=1)
    tenant = jnp.sum(jnp.where(match, session_tenant[None, :], 0), axis=1)
    row = jnp.arange(256, dtype=jnp.int32)
    row_place = (row // 64) % 2
    row_pos = row % 64 + 64 * (row // 128)

    def of(pair, index):
        return jnp.where(index == 0, pair[0], pair[1])

    tmask = (row_pos >= of(total, row_place)) & (row_pos < of(length, row_place))
    keep = (row % 128) < of(length, row // 128)
    tenant_mask = (jnp.arange(128, dtype=jnp.int32) // ADAPTER_RANK)[:, None] == of(tenant, row_place)[None, :]
    return (
        tgt, key, bias, tmask.astype(F32)[:, None], keep.astype(F32)[:, None], tenant_mask.astype(F32)
    )


def on_device(
    patches, vit_qkv, vit_out, merge_weight, query_key_value_weight, adapter_down, adapter_up_weight,
    text_embed, vis_count, image_session, session_slot, session_tenant, session_len,
):
    shard_id = lax.axis_index("seq")
    vit = jnp.concatenate([vit_qkv[0], vit_qkv[1], vit_qkv[2], vit_out.T], axis=1)
    vit = jnp.pad(vit, ((0, 8), (0, 0)))
    maps = layout(shard_id, vis_count, image_session, session_slot, session_len, session_tenant)
    operands = (
        patches.reshape(512, DV), vit, merge_weight, query_key_value_weight.reshape(256, COLS),
        adapter_down, adapter_up_weight.reshape(128, COLS), text_embed,
    ) + maps + tables()
    vmem = pl.BlockSpec(memory_space=pltpu.VMEM)
    hbm = pl.BlockSpec(memory_space=pl.ANY)
    dma = pltpu.SemaphoreType.DMA
    return pl.pallas_call(
        kernel,
        out_shape=jax.ShapeDtypeStruct((256, 1024), F32),
        in_specs=[hbm if i in (2, 3) else vmem for i in range(len(operands))],
        out_specs=vmem,
        scratch_shapes=[
            pltpu.VMEM((1536, 640), BF16),
            pltpu.VMEM((1280, 640), F32),
            pltpu.VMEM((1280, 640), BF16),
            pltpu.VMEM((512, 1280), BF16),
            pltpu.VMEM((512, 1280), BF16),
            pltpu.VMEM((512, 640), BF16),
            pltpu.VMEM((1280, 1280), BF16),
            pltpu.VMEM((1280, 512), BF16),
            pltpu.VMEM((512, 1280), F32),
            pltpu.VMEM((2, 1280, 1024), BF16),
            pltpu.VMEM((128, 1024), F32),
            pltpu.VMEM((512, 256), BF16),
            pltpu.VMEM((512, 256), BF16),
            pltpu.VMEM((2048, 1024), BF16),
            pltpu.VMEM((128, 256), F32),
            pltpu.VMEM((8192, 1280), BF16),
            pltpu.VMEM((256, 1280), F32),
            dma((2,)), dma((4,)), dma((1,)), dma((4,)), dma((4,)), dma((4,)), dma((W_COPIES,)), dma((W_COPIES,)),
            dma((8,)), dma((8,)), dma((8,)), dma((8,)), dma((8,)), dma((8,)), dma((8,)), dma((8,)), dma((8,)), dma((8,)),
            dma((1,)), dma((1,)), dma((1,)), dma((1,)),
        ],
        compiler_params=pltpu.CompilerParams(
            collective_id=0, has_side_effects=True, vmem_limit_bytes=63 * 1024 * 1024
        ),
    )(*operands)


def solution(mesh):
    placed = (
        P("seq", None, None),
        P(None, "seq", "tp"),
        P("tp", "seq"),
        P(None, "tp"),
        P("seq", "tp", None, None),
        P("tp", None),
        P(None, "tp", None, None),
        P("seq", "tp"),
        P(),
        P(),
        P(),
        P(),
        P(),
    )
    return jax.shard_map(
        on_device, mesh=mesh, in_specs=placed, out_specs=P("seq", "tp"), check_vma=False
    )
```

time: 429 us -> 147 us (0.34)
  waiting for transfers between devices: 315 us -> 0 us
  Pallas kernels: 0 us -> 123 us
  blocking collectives: 39 us -> 0 us
  matrix products: 28.2 us -> 0 us
  between operations: 14 us -> 0.08 us
  starting transfers between devices: 12.1 us -> 0 us
    all_gather x4 -> x0, waiting for transfers between devices: 219 us -> none  [the longest x1 98.8 us: on_device(): lax.all_gather(query_key_value_weight, 'seq', axis=0, tiled=True)]
    pallas_call x0 -> x1, Pallas kernels: none -> 123 us  [on_device(): pl.pallas_call(kernel, out_shape=jax.ShapeDtypeStruct((256, 1024), F32),...]
    psum x1 -> x0, waiting for transfers between devices: 47 us -> none  [on_device(): lax.psum((jnp.sum(raw_part * raw_part, axis=1), jnp.dot(tokens_part, adap...]
    reduce_scatter x1 -> x0, waiting for transfers between devices: 39.1 us -> none  [on_device(): lax.psum_scatter(jnp.dot(context, out_enc, preferred_element_type=jnp.flo...]
    dot_general x11 -> x0, matrix products: 28.2 us -> none  [the longest x1 12.2 us: decode_rows(): jnp.dot(normalized_rows, flattened_qkv_weight, preferred_element_type=jnp...]
    all_gather x1 -> x0, blocking collectives: 26.6 us -> none  [on_device(): lax.all_gather(vit_out, 'seq', axis=1, tiled=True)]
    psum x1 -> x0, blocking collectives: 12.5 us -> none  [on_device(): lax.psum((jnp.sum(raw_part * raw_part, axis=1), jnp.dot(tokens_part, adap...]
    all_to_all x1 -> x0, starting transfers between devices: 11.7 us -> none  [on_device(): lax.all_to_all(outgoing, 'seq', split_axis=0, concat_axis=0, tiled=True)]
  transfers between devices with their start and end apart: 7 -> 0, of which waited for: 7 -> 0; matrix products, arithmetic and copies ran while one was open for 2% -> 0% of each run, Pallas kernels for 0% -> 0%
where the time goes in v1:
time: 147 us; the launch traced here: 146 us
  Pallas kernels  123 us (84%)
  other arithmetic  12.7 us (9%)
  local copies, waits for them, and re-layouts  10.3 us (7%)
    pallas_call x1, Pallas kernels, on_device(): pl.pallas_call(kernel, out_shape=jax.ShapeDtypeStruct((256, 1024), F32),...  123 us
    unnamed x3, local copies, waits for them, and re-layouts  4.82 us
    convert_element_type x1, other arithmetic, layout(): tmask.astype(F32)[:, None]  3.14 us

profile of v1, /device:TPU:1, one launch (start us, length us, event | category | flops | bytes accessed | tf_op | source)
XLA Modules:
  0.0 146.2 jit_solution(7173801980665723260)
XLA Ops:
  0.0 0.9 fusion.47
  0.9 0.7 fusion.53
  1.6 1.3 compare_select_fusion.4
  2.9 0.8 select_reduce_fusion
  3.7 0.1 reshape.393
  3.8 0.1 broadcast_in_dim.139
  3.9 0.1 mul.47
  4.0 0.7 add_add_fusion.tgt
  4.7 0.8 reshape.394
  5.4 0.1 fusion.31
  5.5 0.2 select_reduce_fusion.1
  5.7 0.1 fusion.45
  5.9 0.6 fusion.54
  6.4 0.1 broadcast_in_dim.140
  6.5 0.1 reshape.395
  6.6 0.1 broadcast_in_dim.142
  6.6 0.1 reshape.396
  6.7 0.6 fusion.33.key
  7.3 0.1 broadcast_in_dim.145
  7.4 0.1 reshape.397
  7.5 0.8 slice_bitcast_fusion.2
  8.3 1.4 fusion.28.vit
  9.8 0.7 and_select_fusion.bias
  10.5 0.7 compare_convert_fusion.tenant_mask
  11.2 3.1 %fusion.20.tmask = f32[256,1]{1,0:T(8,128)} fusion(s32[]{:T(128)} %bitcast.12, s32[]{:T(128)} %bitcast.11, s32[]{:T(128)} %bitcast.10, s32[]{:T(128)} %bitcast.9), kind=kLoop, calls=%fused_computation.33 | loop fusion | flops 9728 | bytes 1040 | tf_op jit(solution)/shard_map/convert_element_type | solution.py:528
  14.3 1.9 %fusion.21.keep = f32[256,1]{1,0:T(8,128)} fusion(s32[]{:T(128)} %bitcast.12, s32[]{:T(128)} %bitcast.11), kind=kLoop, calls=%fused_computation.34 | loop fusion | flops 4096 | bytes 1032 | tf_op jit(solution)/shard_map/convert_element_type | solution.py:528
  16.3 1.2 copy.30
  17.4 0.9 copy.32.up
  18.4 1.3 copy.29
  19.7 1.1 copy.31.w
  20.8 123.1 %shard_map.172 = f32[256,1024]{1,0:T(8,128)} custom-call(bf16[512,1280]{1,0:T(8,128)(2,1)} %bitcast.29, bf16[48,640]{1,0:T(8,128)(2,1)} %fusion.28.vit, bf16[5120,1024]{1,0:T(8,128)(2,1)} %mw.1, bf16[256,1280]{1,0:T(8,128)(2,1)} %copy.31.w, bf16[1024,128]{1,0:T(8,128)(2,1)} %down.1, bf16[128,1280]{1,0:T(8,128)(2,1)} %copy.32.up, bf16[256,1024]{1,0:T(8,128)(2,1)} %text.1, ...), custom_call_target="tpu_custom_call" | custom-call | tf_op jit(solution)/shard_map/pallas_call | solution.py:547
  143.9 2.3 %copy.34 = f32[256,1024]{1,0:T(8,128)} copy(f32[256,1024]{1,0:T(8,128)} %shard_map.172) | data formatting | bytes 2097152
  (10 shorter events, 0.1 us)

commit v2 on v1

v2 whole, which is shorter than its diff:
```python
import functools
import math

import jax
import jax.numpy as jnp
import numpy as np
from jax import lax
from jax.experimental import pallas as pl
from jax.experimental.pallas import tpu as pltpu
from jax.sharding import PartitionSpec as P

DV = 1280
HV = 16
HEAD = 80
DECODER_WIDTH = 8192
DECODER_HEAD_DIM = 128
ADAPTER_RANK = 16
IMG_DEV = 32
VMAX = 4
SLOT = 128
QUERY_PER_KEY = 8
N_SEQ = 32
N_TP = 8
COLS = 1280
EPSILON = 1e-06
ROPE_BASE = 1000000.0
MESH = pl.DeviceIdType.MESH
F32 = jnp.float32
BF16 = jnp.bfloat16


def tables():
    perm = np.zeros((512, 512), np.float32)
    for j in range(4):
        for i in range(32):
            for m in range(4):
                perm[j * 128 + i * 4 + m, i * 16 + m * 4 + j] = 1
    select = np.zeros((512, 768), np.float32)
    for group in range(6):
        for lane in range(HEAD):
            select[group * HEAD + lane, group * 128 + lane] = 1
    select_out = np.zeros((160, 640), np.float32)
    for row in range(160):
        select_out[row, 480 + row] = 1
    half = DECODER_HEAD_DIM // 2
    inverse_freq = np.power(
        np.float32(ROPE_BASE), -(np.arange(half, dtype=np.float32) * 2.0 / DECODER_HEAD_DIM)
    ).astype(np.float32)
    angles = np.arange(SLOT, dtype=np.float32)[:, None] * inverse_freq[None, :]
    cosine = np.cos(angles).astype(np.float32)
    sine = np.sin(angles).astype(np.float32)
    return (
        jnp.asarray(perm, BF16),
        jnp.asarray(select, BF16),
        jnp.asarray(select_out, BF16),
        jnp.asarray(np.concatenate([cosine, cosine], 1)),
        jnp.asarray(np.concatenate([-sine, sine], 1)),
    )


def plane_copies(size, cut, opposite):
    whole, first, second = (0, size), (0, cut), (cut, size - cut)

    def sib(blocks):
        return [(by, bx, 0, size, 0, 0, True) for by, bx in blocks]

    def go(by, bx, part, ty, tx):
        return (by, bx, part[0], part[1], ty, tx, False)

    stage0 = [go(0, 0, whole, 0, 1), go(0, 0, whole, 0, -1), go(0, 0, whole, 1, 0), go(0, 0, whole, -1, 0)]
    stage0 += sib([(0, 0)])
    stage1 = [
        go(0, -1, first, 0, 1), go(0, 1, second, 0, -1), go(-1, 0, first, 1, 0), go(1, 0, second, -1, 0),
    ]
    for side in (-1, 1):
        for to in (-1, 1):
            stage1 += [go(0, side, first, to, 0), go(side, 0, second, 0, to)]
    stage1 += sib([(0, -1), (0, 1), (-1, 0), (1, 0)])
    stage2 = [
        go(0, 2, first, 1, 0), go(0, 2, first, -1, 0), go(2, 0, second, 0, 1), go(2, 0, second, 0, -1),
        go(-1, 1, first, 1, 0), go(1, -1, first, -1, 0), go(1, -1, second, 0, 1), go(-1, 1, second, 0, -1),
    ]
    stage2 += sib([(0, 2), (2, 0), (-1, -1), (-1, 1), (1, -1), (1, 1)])
    ways = ((-1, 2, 1, 0), (1, 2, -1, 0), (2, -1, 0, 1), (2, 1, 0, -1))
    stage3 = [go(by, bx, part, ty, tx) for (by, bx, ty, tx), part in zip(ways, opposite) if part is not None]
    stage3 += sib([(-1, 2), (1, 2), (2, -1), (2, 1)])
    stage4 = sib([(2, 2)])
    stages, count = [], 0
    for stage in (stage0, stage1, stage2, stage3, stage4):
        stages.append([(count + i,) + entry for i, entry in enumerate(stage)])
        count += len(stage)
    return stages, count


W_STAGES, W_COPIES = plane_copies(256, 128, ((0, 64), (64, 64), (128, 64), (192, 64)))
G_STAGES, G_COPIES = plane_copies(48, 32, ((0, 16), (16, 16), (32, 16), None))


def bdot(a, b):
    return jnp.dot(a, b, preferred_element_type=F32)


def bdot_nt(a, b):
    return lax.dot_general(a, b, (((1,), (1,)), ((), ())), preferred_element_type=F32)


def normalize(values):
    mean_val = jnp.mean(values, axis=-1, keepdims=True)
    centered = values - mean_val
    variance = jnp.mean(centered * centered, axis=-1, keepdims=True)
    return centered * lax.rsqrt(variance + EPSILON)


def iota(shape, axis):
    return lax.broadcasted_iota(jnp.int32, shape, axis)


def one_hot(mask):
    return mask.astype(F32).astype(BF16)


def kernel(
    slot_ref, tenant_ref, len_ref, counts, sessions,
    patches, vit_qkv, vit_out, mw, w, down, up, text, perm, select, select_out, cosine, sine,
    out,
    g, wf, wall, pp, ln, qkv, o_all, ctx_all, enc, mwb, vis, xs, ys, tok, dl, w_all, up_all, acc,
    mw_sem, gs_sem, gr_sem, ws_sem, wr_sem,
    os_sem, or_sem, ofs_sem, ofr_sem, cs_sem, cr_sem, es_sem, er_sem, ls_sem, lr_sem,
    as_sem, ar_sem, ds_sem, dr_sem,
):
    s = lax.axis_index("seq")
    t = lax.axis_index("tp")
    core = lax.rem(s, 2)
    chip = s // 2
    cx = lax.rem(chip, 4)
    cy = chip // 4
    sibling = s + 1 - 2 * core

    def chip_at(dy, dx):
        return lax.rem(cy + (dy + 4), 4) * 4 + lax.rem(cx + (dx + 4), 4)

    def rows(ref, start, size, step=16):
        return ref.at[pl.ds(pl.multiple_of(start, step), size)]

    def arrived(ref, sem):
        pltpu.make_async_copy(ref, ref, sem).wait()

    barrier = pltpu.get_barrier_semaphore()

    def greet_seq(i, carry):
        pl.semaphore_signal(barrier, inc=1, device_id=(lax.rem(s + i, N_SEQ), t), device_id_type=MESH)
        return carry

    def greet_tp(i, carry):
        pl.semaphore_signal(barrier, inc=1, device_id=(s, lax.rem(t + i, N_TP)), device_id_type=MESH)
        return carry

    lax.fori_loop(1, N_SEQ, greet_seq, 0)
    lax.fori_loop(1, N_TP, greet_tp, 0)

    mw_load = pltpu.make_async_copy(mw, mwb, mw_sem.at[0])
    mw_load.start()

    def plane(stages, ref, send, recv):
        def start(stage):
            for index, by, bx, first, size, ty, tx, sib in stages[stage]:
                piece = ref(core, chip_at(by, bx), first, size)
                pltpu.make_async_remote_copy(
                    src_ref=piece, dst_ref=piece, send_sem=send.at[index], recv_sem=recv.at[index],
                    device_id=(sibling if sib else chip_at(ty, tx) * 2 + core, t), device_id_type=MESH,
                ).start()

        def wait(stage):
            for index, by, bx, first, size, ty, tx, sib in stages[stage]:
                if not sib:
                    arrived(ref(core, chip_at(by - ty, bx - tx), first, size), recv.at[index])

        def rest():
            for stage in stages:
                for index, by, bx, first, size, ty, tx, sib in stage:
                    if sib:
                        arrived(ref(1 - core, chip_at(by, bx), first, size), recv.at[index])

        def sent():
            for stage in stages:
                for index, by, bx, first, size, ty, tx, sib in stage:
                    arrived(ref(core, chip_at(by, bx), first, size), send.at[index])

        return start, wait, rest, sent

    g_start, g_wait, g_rest, g_sent = plane(
        G_STAGES, lambda c, at, first, size: rows(g, (c * 16 + at) * 48 + first, size), gs_sem, gr_sem
    )
    w_start, w_wait, w_rest, w_sent = plane(
        W_STAGES, lambda c, at, first, size: rows(w_all, (at * 2 + c) * 256 + first, size), ws_sem, wr_sem
    )

    right = (s, lax.rem(t + 1, N_TP))
    left = (s, lax.rem(t + N_TP - 1, N_TP))

    def ring(buf, base, size, cut, send, recv):
        def part(way, origin, k):
            first = base(lax.rem(origin + 2 * N_TP, N_TP))
            if k < 3:
                return rows(buf, first, size)
            if way == 0:
                return rows(buf, first, cut)
            return rows(buf, first + cut, size - cut)

        def start(k):
            for way, to, origin in ((0, right, t - k), (1, left, t + k)):
                piece = part(way, origin, k)
                pltpu.make_async_remote_copy(
                    src_ref=piece, dst_ref=piece, send_sem=send.at[way * 4 + k], recv_sem=recv.at[way * 4 + k],
                    device_id=to, device_id_type=MESH,
                ).start()

        def wait(k):
            arrived(part(0, t - 1 - k, k), recv.at[k])
            arrived(part(1, t + 1 + k, k), recv.at[4 + k])

        def sent():
            for k in range(4):
                arrived(part(0, t - k, k), send.at[k])
                arrived(part(1, t + k, k), send.at[4 + k])

        return start, wait, sent

    e_start, e_wait, e_sent = ring(tok, lambda z: z * 256 + 128, 128, 64, es_sem, er_sem)
    l_start, l_wait, l_sent = ring(tok, lambda z: z * 256, 128, 64, ls_sem, lr_sem)
    o_start, o_wait, o_sent = ring(o_all, lambda z: z * 160 + 80 * core, 80, 48, os_sem, or_sem)
    c_start, c_wait, c_sent = ring(ctx_all, lambda z: z * 160, 160, 80, cs_sem, cr_sem)

    def o_pieces(k, c):
        origins = [(0, t - 1 - k), (1, t + 1 + k)] if k < 3 else [(0, t + 4)]
        for way, origin in origins:
            yield way * 4 + k, rows(o_all, lax.rem(origin + 2 * N_TP, N_TP) * 160 + 80 * c, 80)

    def o_share(k):
        for index, piece in o_pieces(k, core):
            pltpu.make_async_remote_copy(
                src_ref=piece, dst_ref=piece, send_sem=ofs_sem.at[index], recv_sem=ofr_sem.at[index],
                device_id=(sibling, t), device_id_type=MESH,
            ).start()

    def o_shared(k, sems, c):
        for index, piece in o_pieces(k, c):
            arrived(piece, sems.at[index])

    r_640, c_640 = iota((160, 640), 0), iota((160, 640), 1)
    mine = jnp.zeros((40, 640), F32)
    for j in range(3):
        mine += bdot(vit_qkv[j], one_hot(c_640 == r_640 + 160 * j))
    mine += lax.dot_general(
        vit_out[...], one_hot(c_640 == r_640 + 480), (((0,), (0,)), ((), ())), preferred_element_type=F32
    )
    own_g = pl.ds(pl.multiple_of((core * 16 + chip) * 48, 16), 48)
    g[own_g, :] = jnp.concatenate([mine, jnp.zeros((8, 640), F32)], axis=0).astype(BF16)

    def look_up(k, carry):
        slots, len0, len1, tenant0, tenant1 = carry
        slot = slot_ref[k]
        slots = jnp.where(sessions[...] == k, slot, slots)
        at0, at1 = slot == 2 * s, slot == 2 * s + 1
        return (
            slots, jnp.where(at0, len_ref[k], len0), jnp.where(at1, len_ref[k], len1),
            jnp.where(at0, tenant_ref[k], tenant0), jnp.where(at1, tenant_ref[k], tenant1),
        )

    zero = jnp.int32(0)
    slots, len0, len1, tenant0, tenant1 = lax.fori_loop(
        0, 64, look_up, (jnp.zeros((8, 128), jnp.int32), zero, zero, zero, zero)
    )
    length = (len0, len1)

    pl.semaphore_wait(barrier, N_SEQ + N_TP - 2)
    g_start(0)

    own_tok = pl.multiple_of(t * 256, 256)
    for l in range(2):
        tok[pl.ds(own_tok + 128 + 64 * l, 64), :] = jnp.where(
            iota((64, 1024), 0) + 64 < length[l], text[128 * l + 64:128 * l + 128, :], jnp.zeros((64, 1024), BF16)
        )
    e_start(0)

    for n in range(5):
        lanes = slice(256 * n, 256 * n + 256)
        pp[:, lanes] = bdot(perm[...], patches[:, lanes]).astype(BF16)

    g_wait(0)
    g_start(1)
    for r in range(4):
        part = slice(128 * r, 128 * r + 128)
        ln[part, :] = normalize(pp[part, :].astype(F32)).astype(BF16)

    here = (slots >> 1) == s
    folded = jnp.concatenate(
        [jnp.where(here, counts[...], 0).astype(F32), jnp.where(here, slots & 1, 0).astype(F32)], axis=0
    ).astype(BF16)
    spread = bdot(folded, one_hot((iota((128, 512), 0) >> 5) == ((iota((128, 512), 1) >> 4) & 3)))
    n_8 = iota((8, 512), 1)
    own_row = iota((8, 512), 0) == (n_8 >> 6)
    count_n = jnp.sum(jnp.where(own_row, spread[:8, :], 0.0), axis=0, keepdims=True)
    place_n = jnp.sum(jnp.where(own_row, spread[8:, :], 0.0), axis=0, keepdims=True)
    by_place = jnp.where(iota((8, 512), 0) == place_n.astype(jnp.int32), count_n, 0.0)
    n_from, n_to = iota((512, 512), 0), iota((512, 512), 1)
    before = bdot(by_place.astype(BF16), one_hot(((n_from & 15) == 0) & ((n_from >> 4) < (n_to >> 4))))
    offset_n = jnp.where(place_n > 0.5, before[1:2, :], before[0:1, :])
    visual_rows = jnp.sum(by_place, axis=1, keepdims=True) * (1.0 / 16.0)
    n_1 = n_8[0:1, :]
    row_n = jnp.where(
        (n_1 & 3).astype(F32) < count_n, place_n * 64.0 + offset_n + (n_1 & 3).astype(F32), -1.0
    ).astype(jnp.int32)

    lane_8 = iota((128, 128), 1)
    encoded_here = bdot(
        jnp.concatenate([slots.astype(F32), counts[...].astype(F32)], axis=0).astype(BF16),
        one_hot(iota((128, 128), 0) == lax.rem(s, 4) * 32 + (lane_8 >> 2)),
    )
    own_row = iota((8, 128), 0) == s // 4
    slot_c = jnp.sum(jnp.where(own_row, encoded_here[:8, :], 0.0), axis=0, keepdims=True).astype(jnp.int32)
    count_c = jnp.sum(jnp.where(own_row, encoded_here[8:, :], 0.0), axis=0, keepdims=True).astype(jnp.int32)
    target_c = (slot_c >> 1) * 16 + (lane_8[0:1, :] & 3)
    key_8 = iota((128, 128), 0)
    bias = jnp.where(((key_8 >> 2) == (lane_8 >> 2)) & ((key_8 & 3) < count_c), 0.0, -1e30)
    tenant_mask = (
        (iota((128, 256), 0) >> 4) == jnp.where((iota((128, 256), 1) & 64) == 0, tenant0, tenant1)
    ).astype(F32)

    g_wait(1)
    g_start(2)
    own_w = pl.ds(pl.multiple_of(s * 256, 256), 256)
    for j in range(10):
        w_all[own_w, 128 * j:128 * j + 128] = w[:, j, :]
    e_wait(0)
    e_start(1)
    g_wait(2)
    g_start(3)
    w_start(0)
    for j in range(10):
        up_all[:, 128 * j:128 * j + 128] = up[:, j, :]
    g_wait(3)
    g_start(4)
    g_rest()

    for c in range(4):
        for b in range(8):
            first = ((b % 2) * 16 + 4 * c + b // 2) * 48
            wf[40 * b:40 * b + 40, :] = g[first:first + 48, :].astype(F32)[:40, :]
        wall[320 * c:320 * c + 320, :] = wf[...].astype(BF16)
    own_o = pl.multiple_of(t * 160, 32)
    for r in range(5):
        part = slice(256 * r, 256 * r + 256)
        o_all[pl.ds(own_o, 160), part] = bdot_nt(select_out[...], wall[part, :]).astype(BF16)
    o_start(0)

    for n in range(2):
        lanes = slice(256 * n, 256 * n + 256)
        qkv[:, lanes] = bdot(ln[...], wall[:, lanes]).astype(BF16)
    scale = 1.0 / math.sqrt(HEAD)
    for h in range(2):
        q_h = bdot(qkv[...], select[:, 128 * h:128 * h + 128]).astype(BF16)
        k_h = bdot(qkv[...], select[:, 256 + 128 * h:384 + 128 * h]).astype(BF16)
        v_h = bdot(qkv[...], select[:, 512 + 128 * h:640 + 128 * h])
        v_t = jnp.transpose(v_h).astype(BF16)
        for q in range(4):
            scores = bdot_nt(k_h, q_h[128 * q:128 * q + 128, :]) * scale
            scores = scores.reshape(4, 128, 128) + bias[None]
            largest = jnp.max(jnp.max(scores, axis=0), axis=0, keepdims=True)
            exponent = jnp.exp(scores - largest[None])
            total = jnp.sum(jnp.sum(exponent, axis=0), axis=0, keepdims=True)
            probs = (exponent / total[None]).astype(BF16).reshape(512, 128)
            ctx_t = bdot(v_t, probs).astype(BF16)
            ctx_all[pl.ds(own_o + 80 * h, 80), 128 * q:128 * q + 128] = ctx_t[:80, :]
    c_start(0)

    def project_out(z, first=False):
        at = pl.ds(pl.multiple_of(lax.rem(z + 2 * N_TP, N_TP) * 160, 32), 160)
        for n in range(5):
            lanes = slice(256 * n, 256 * n + 256)
            term = lax.dot_general(
                ctx_all[at, :], o_all[at, lanes], (((0,), (0,)), ((), ())), preferred_element_type=F32
            )
            enc[:, lanes] = (pp[:, lanes].astype(F32) if first else enc[:, lanes]) + term

    o_wait(0)
    o_start(1)
    o_share(0)
    project_out(t, True)
    c_wait(0)
    c_start(1)
    o_wait(1)
    o_start(2)
    o_share(1)
    w_wait(0)
    w_start(1)
    o_shared(0, ofr_sem, 1 - core)
    project_out(t - 1)
    project_out(t + 1)
    c_wait(1)
    c_start(2)
    o_wait(2)
    o_start(3)
    o_share(2)
    o_shared(1, ofr_sem, 1 - core)
    project_out(t - 2)
    project_out(t + 2)
    c_wait(2)
    c_start(3)
    o_wait(3)
    o_share(3)
    o_shared(2, ofr_sem, 1 - core)
    e_wait(1)
    e_start(2)
    project_out(t - 3)
    project_out(t + 3)
    o_shared(3, ofr_sem, 1 - core)
    mw_load.wait()
    c_wait(3)
    project_out(t + 4)

    merged = jnp.zeros((128, 1024), F32)
    for j in range(4):
        merged_in = normalize(enc[128 * j:128 * j + 128, :]).astype(BF16)
        merged += bdot(merged_in, mwb[1280 * j:1280 * j + 1280, :])
    vis[...] = merged.astype(BF16)

    row_512 = iota((512, 128), 0)
    outgoing = jnp.zeros((512, 256), F32)
    for q in range(4):
        outgoing += bdot(one_hot(row_512 == target_c + 4 * q), vis[:, 256 * q:256 * q + 256])
    xs[...] = outgoing.astype(BF16)

    def send_rows(i, carry):
        to = lax.rem(s + i, N_SEQ)
        pltpu.make_async_remote_copy(
            src_ref=rows(xs, to * 16, 16), dst_ref=rows(ys, s * 16, 16),
            send_sem=as_sem.at[0], recv_sem=ar_sem.at[0], device_id=(to, t), device_id_type=MESH,
        ).start()
        return carry

    lax.fori_loop(1, N_SEQ, send_rows, 0)
    own_y = pl.ds(pl.multiple_of(s * 16, 16), 16)
    ys[own_y, :] = xs[own_y, :]
    w_wait(1)
    w_start(2)
    e_wait(2)
    e_start(3)
    arrived(ys.at[pl.ds(0, 496)], ar_sem.at[0])

    row_128 = iota((128, 512), 0)
    position = iota((64, 256), 0)
    for q in range(4):
        lanes = slice(256 * q, 256 * q + 256)
        picked = bdot(one_hot((row_128 == row_n) & (((n_1 >> 2) & 3) == q)), ys[...]).astype(BF16)
        for l in range(2):
            is_text = (position.astype(F32) >= visual_rows[l:l + 1, :]) & (position < length[l])
            tok[pl.ds(own_tok + 64 * l, 64), lanes] = jnp.where(
                is_text, text[128 * l:128 * l + 64, lanes], picked[64 * l:64 * l + 64, :]
            )
    l_start(0)

    down_sums = jnp.transpose(bdot(tok[pl.ds(own_tok, 256), :], down[...])) * tenant_mask
    dl[pl.ds(pl.multiple_of(t * 16, 16), 16), :] = jnp.sum(down_sums.reshape(8, 16, 256), axis=0)

    def send_down(i, carry):
        piece = rows(dl, t * 16, 16)
        pltpu.make_async_remote_copy(
            src_ref=piece, dst_ref=piece, send_sem=ds_sem.at[0], recv_sem=dr_sem.at[0],
            device_id=(s, lax.rem(t + i, N_TP)), device_id_type=MESH,
        ).start()
        return carry

    lax.fori_loop(1, N_TP, send_down, 0)

    l_wait(0)
    l_start(1)
    w_wait(2)
    w_start(3)
    l_wait(1)
    l_start(2)
    e_wait(3)
    w_wait(3)
    w_start(4)
    w_rest()

    def project(z):
        x = tok[pl.ds(pl.multiple_of(z * 256, 256), 256), :]
        first = pl.multiple_of(z * 1024, 1024)
        for n in range(5):
            lanes = slice(256 * n, 256 * n + 256)
            acc[:, lanes] += bdot(x, w_all[pl.ds(first, 1024), lanes])
        x_wide = x.astype(F32)
        return jnp.sum(x_wide * x_wide, axis=1, keepdims=True)

    acc[...] = jnp.zeros_like(acc)
    squares = project(t)
    squares += project(lax.rem(t + 1, N_TP))
    squares += project(lax.rem(t + 7, N_TP))
    l_wait(2)
    l_start(3)
    for k in (2, 6, 3, 5):
        squares += project(lax.rem(t + k, N_TP))
    arrived(dl.at[pl.ds(0, 112)], dr_sem.at[0])
    down_t = jnp.sum(dl[...].reshape(8, 16, 256), axis=0)
    lora = jnp.transpose(jnp.concatenate([down_t] * 8, axis=0) * tenant_mask).astype(BF16)
    acc[...] += bdot(lora, up_all[...])
    l_wait(3)
    squares += project(lax.rem(t + 4, N_TP))
    inverse = lax.rsqrt(squares * (1.0 / DECODER_WIDTH) + EPSILON)

    causal = iota((128, 128), 0) >= iota((128, 128), 1)
    ones = jnp.ones((128, 128), BF16)
    for l in range(2):
        low, high = slice(64 * l, 64 * l + 64), slice(128 + 64 * l, 192 + 64 * l)
        factor = jnp.concatenate([inverse[low, :], inverse[high, :]], axis=0)

        def column(index):
            lanes = slice(128 * index, 128 * index + 128)
            return jnp.concatenate([acc[low, lanes], acc[high, lanes]], axis=0) * factor

        def rotate(values):
            return values * cosine[...] + pltpu.roll(values, 64, 1) * sine[...]

        key_rows = rotate(column(8)).astype(BF16)
        value_rows = jnp.concatenate([column(9).astype(BF16), ones], axis=1)
        kept = iota((128, 128), 0) < length[l]
        for j in range(QUERY_PER_KEY):
            query = rotate(column(j)).astype(BF16)
            scores = bdot_nt(query, key_rows) * (1.0 / math.sqrt(DECODER_HEAD_DIM))
            scores = jnp.where(causal, scores, -1e30)
            exponent = jnp.exp(scores - jnp.max(scores, axis=1, keepdims=True)).astype(BF16)
            summed = bdot(exponent, value_rows)
            out[128 * l:128 * l + 128, 128 * j:128 * j + 128] = jnp.where(
                kept, summed[:, :128] / summed[:, 128:], 0.0
            )

    g_sent()
    w_sent()
    e_sent()
    l_sent()
    o_sent()
    c_sent()
    for k in range(4):
        o_shared(k, ofs_sem, core)
    arrived(xs.at[pl.ds(0, 496)], as_sem.at[0])
    arrived(dl.at[pl.ds(0, 112)], ds_sem.at[0])


def on_device(
    patches, vit_qkv, vit_out, merge_weight, query_key_value_weight, adapter_down, adapter_up_weight,
    text_embed, vis_count, image_session, session_slot, session_tenant, session_len,
):
    operands = (
        session_slot, session_tenant, session_len, vis_count.reshape(8, 128), image_session.reshape(8, 128),
        patches.reshape(512, DV), vit_qkv, vit_out, merge_weight,
        query_key_value_weight.reshape(256, 10, 128), adapter_down, adapter_up_weight.reshape(128, 10, 128), text_embed,
    ) + tables()
    vmem = pl.BlockSpec(memory_space=pltpu.VMEM)
    smem = pl.BlockSpec(memory_space=pltpu.SMEM)
    hbm = pl.BlockSpec(memory_space=pl.ANY)
    dma = pltpu.SemaphoreType.DMA
    return pl.pallas_call(
        kernel,
        out_shape=jax.ShapeDtypeStruct((256, 1024), F32),
        in_specs=[smem if i < 3 else hbm if i == 8 else vmem for i in range(len(operands))],
        out_specs=vmem,
        scratch_shapes=[
            pltpu.VMEM((1536, 640), BF16),
            pltpu.VMEM((320, 640), F32),
            pltpu.VMEM((1280, 640), BF16),
            pltpu.VMEM((512, 1280), BF16),
            pltpu.VMEM((512, 1280), BF16),
            pltpu.VMEM((512, 512), BF16),
            pltpu.VMEM((1280, 1280), BF16),
            pltpu.VMEM((1280, 512), BF16),
            pltpu.VMEM((512, 1280), F32),
            pltpu.VMEM((5120, 1024), BF16),
            pltpu.VMEM((128, 1024), BF16),
            pltpu.VMEM((512, 256), BF16),
            pltpu.VMEM((512, 256), BF16),
            pltpu.VMEM((2048, 1024), BF16),
            pltpu.VMEM((128, 256), F32),
            pltpu.VMEM((8192, 1280), BF16),
            pltpu.VMEM((128, 1280), BF16),
            pltpu.VMEM((256, 1280), F32),
            dma((1,)), dma((G_COPIES,)), dma((G_COPIES,)), dma((W_COPIES,)), dma((W_COPIES,)),
            dma((8,)), dma((8,)), dma((8,)), dma((8,)), dma((8,)), dma((8,)), dma((8,)), dma((8,)), dma((8,)), dma((8,)),
            dma((1,)), dma((1,)), dma((1,)), dma((1,)),
        ],
        compiler_params=pltpu.CompilerParams(
            collective_id=0, has_side_effects=True, vmem_limit_bytes=64 * 1024 * 1024
        ),
    )(*operands)


def solution(mesh):
    placed = (
        P("seq", None, None),
        P(None, "seq", "tp"),
        P("tp", "seq"),
        P(None, "tp"),
        P("seq", "tp", None, None),
        P("tp", None),
        P(None, "tp", None, None),
        P("seq", "tp"),
        P(),
        P(),
        P(),
        P(),
        P(),
    )
    return jax.shard_map(
        on_device, mesh=mesh, in_specs=placed, out_specs=P("seq", "tp"), check_vma=False
    )
```

time: 147 us -> 122 us (0.83)
  other arithmetic: 12.7 us -> 0 us
  Pallas kernels: 123 us -> 113 us
  local copies, waits for them, and re-layouts: 10.3 us -> 8.3 us
    pallas_call x1, Pallas kernels: 123 us -> 113 us  [on_device(): pl.pallas_call(kernel, out_shape=jax.ShapeDtypeStruct((256, 1024), F32),...]
    convert_element_type x3 -> x0, other arithmetic: 5.78 us -> none  [the longest x1 3.14 us: layout(): tmask.astype(F32)[:, None]]
    unnamed x3 -> x4, local copies, waits for them, and re-layouts: 4.82 us -> 8.3 us
    reshape x7 -> x0, local copies, waits for them, and re-layouts: 3.1 us -> none  [the longest x1 1.08 us: on_device(): query_key_value_weight.reshape(256, COLS)]
    select_n x6 -> x0, other arithmetic: 2.63 us -> none  [the longest x1 1.28 us: of(): return jnp.where(index == 0, pair[0], pair[1])]
    reduce_sum x5 -> x0, other arithmetic: 2.13 us -> none  [the longest x1 0.9 us: layout(): tenant = jnp.sum(jnp.where(match, session_tenant[None, :], 0), axis=1)]
where the time goes in v2:
time: 122 us
  Pallas kernels  113 us (93%)
  local copies, waits for them, and re-layouts  8.3 us (7%)
    pallas_call x1, Pallas kernels, on_device(): pl.pallas_call(kernel, out_shape=jax.ShapeDtypeStruct((256, 1024), F32),...  113 us
    unnamed x4, local copies, waits for them, and re-layouts  8.3 us

profile of v2, /device:TPU:1, one launch (start us, length us, event | category | flops | bytes accessed | tf_op | source)
XLA Modules:
  0.0 121.8 jit_solution(5470370980661278607)
XLA Ops:
  0.0 1.4 %copy.21.vit_out = bf16[160,40]{1,0:T(8,128)(2,1)} copy(bf16[160,40]{0,1:T(8,128)(2,1)} %param.20) | data formatting | bytes 25600 | tf_op args[2]
  1.4 2.0 %copy.25 = bf16[128,1,10,128]{3,2,0,1:T(8,128)(2,1)} copy(bf16[128,1,10,128]{3,0,2,1:T(8,128)(2,1)} %param.24) | data formatting | bytes 655360 | tf_op args[6]
  3.5 2.5 %copy.24 = bf16[256,1,10,128]{3,2,0,1:T(8,128)(2,1)} copy(bf16[256,1,10,128]{3,0,2,1:T(8,128)(2,1)} %param.22) | data formatting | bytes 1310720 | tf_op args[4]
  6.0 113.4 %shard_map.172 = f32[256,1024]{1,0:T(8,128)} custom-call(s32[64]{0:T(128)} %slot_ref.1, s32[64]{0:T(128)} %tenant_ref.1, s32[64]{0:T(128)} %len_ref.1, s32[8,128]{1,0:T(8,128)} %bitcast.12, s32[8,128]{1,0:T(8,128)} %bitcast.13, bf16[512,1280]{1,0:T(8,128)(2,1)} %bitcast.11, bf16[3,40,160]{2,1,0:T(8,128)(2,1)} %vit_qkv.1, bf16[160,40]{1,0:T(8,128)(2,1)} %copy.21.vit_out, ...), custom_call_target="tpu_custom_call" | custom-call | tf_op jit(solution)/shard_map/pallas_call | solution.py:563
  119.5 2.3 %copy.27 = f32[256,1024]{1,0:T(8,128)} copy(f32[256,1024]{1,0:T(8,128)} %shard_map.172) | data formatting | bytes 2097152

commit v3 on v2

v3 whole, which is shorter than its diff:
```python
import functools
import math

import jax
import jax.numpy as jnp
import numpy as np
from jax import lax
from jax.experimental import pallas as pl
from jax.experimental.pallas import tpu as pltpu
from jax.sharding import PartitionSpec as P

DV = 1280
HV = 16
HEAD = 80
DECODER_WIDTH = 8192
DECODER_HEAD_DIM = 128
ADAPTER_RANK = 16
IMG_DEV = 32
VMAX = 4
SLOT = 128
QUERY_PER_KEY = 8
N_SEQ = 32
N_TP = 8
COLS = 1280
EPSILON = 1e-06
ROPE_BASE = 1000000.0
MESH = pl.DeviceIdType.MESH
F32 = jnp.float32
BF16 = jnp.bfloat16


def tables():
    perm = np.zeros((512, 512), np.float32)
    for j in range(4):
        for i in range(32):
            for m in range(4):
                perm[j * 128 + i * 4 + m, i * 16 + m * 4 + j] = 1
    select = np.zeros((512, 768), np.float32)
    for group in range(6):
        for lane in range(HEAD):
            select[32 + group * HEAD + lane, group * 128 + lane] = 1
    half = DECODER_HEAD_DIM // 2
    inverse_freq = np.power(
        np.float32(ROPE_BASE), -(np.arange(half, dtype=np.float32) * 2.0 / DECODER_HEAD_DIM)
    ).astype(np.float32)
    angles = np.arange(SLOT, dtype=np.float32)[:, None] * inverse_freq[None, :]
    cosine = np.cos(angles).astype(np.float32)
    sine = np.sin(angles).astype(np.float32)
    return (
        jnp.asarray(perm, BF16),
        jnp.asarray(select, BF16),
        jnp.asarray(np.concatenate([cosine, cosine], 1)),
        jnp.asarray(np.concatenate([-sine, sine], 1)),
    )


def plane_copies():
    part_a, part_b = (0, 128), (128, 128)

    def sib(blocks):
        return [(by, bx, 0, 256, 0, 0, True) for by, bx in blocks]

    def go(by, bx, part, ty, tx):
        return (by, bx, part[0], part[1], ty, tx, False)

    sides = (-1, 1)
    near = [(0, -1), (0, 1), (-1, 0), (1, 0)]
    lists = {
        "0a": [go(0, 0, part_a, ty, tx) for ty, tx in near],
        "0b": [go(0, 0, part_b, ty, tx) for ty, tx in near],
        "0s": sib([(0, 0)]),
        "1a": [go(0, -1, part_a, 0, 1), go(-1, 0, part_a, 1, 0)]
        + [go(0, side, part_a, to, 0) for side in sides for to in sides],
        "1b": [go(0, 1, part_b, 0, -1), go(1, 0, part_b, -1, 0)]
        + [go(side, 0, part_b, 0, to) for side in sides for to in sides],
        "1s": sib(near),
        "2a": [go(0, 2, part_a, 1, 0), go(0, 2, part_a, -1, 0), go(-1, 1, part_a, 1, 0), go(1, -1, part_a, -1, 0)],
        "2b": [go(2, 0, part_b, 0, 1), go(2, 0, part_b, 0, -1), go(1, -1, part_b, 0, 1), go(-1, 1, part_b, 0, -1)],
        "2s": sib([(0, 2), (2, 0), (-1, -1), (-1, 1), (1, -1), (1, 1)]),
        "3a": [go(-1, 2, (0, 64), 1, 0), go(1, 2, (64, 64), -1, 0)],
        "3b": [go(2, -1, (128, 64), 0, 1), go(2, 1, (192, 64), 0, -1)],
        "3s": sib([(-1, 2), (1, 2), (2, -1), (2, 1)]),
        "4s": sib([(2, 2)]),
    }
    return {
        name: (i, sum(entry[3] for entry in entries), entries) for i, (name, entries) in enumerate(lists.items())
    }


W_GROUPS = plane_copies()
LANES = (256, 384)


def bdot(a, b):
    return jnp.dot(a, b, preferred_element_type=F32)


def bdot_nt(a, b):
    return lax.dot_general(a, b, (((1,), (1,)), ((), ())), preferred_element_type=F32)


def normalize(values):
    mean_val = jnp.mean(values, axis=-1, keepdims=True)
    centered = values - mean_val
    variance = jnp.mean(centered * centered, axis=-1, keepdims=True)
    return centered * lax.rsqrt(variance + EPSILON)


def iota(shape, axis):
    return lax.broadcasted_iota(jnp.int32, shape, axis)


def one_hot(mask):
    return mask.astype(F32).astype(BF16)


def kernel(
    slot_ref, tenant_ref, len_ref, counts, sessions, vit_qkv, vit_out,
    patches_hbm, mw, w, down_hbm, up, text_hbm, perm_hbm, select_hbm, cosine_hbm, sine_hbm,
    out,
    patches, down, text, perm, select, cosine, sine, w_in, up_in,
    g0, g1, wf, wall, pp, ln, qkv, o_all, ctx_all, enc, mwb, vis, xs, ys, tok, dl, w_all, up_all, acc, squares, res,
    load_sem, gs_sem, gr_sem, fs_sem, fr_sem, ws_sem, wr_sem,
    os_sem, or_sem, ofs_sem, ofr_sem, cs_sem, cr_sem, es_sem, er_sem, ls_sem, lr_sem,
    as_sem, ar_sem, ds_sem, dr_sem,
):
    s = lax.axis_index("seq")
    t = lax.axis_index("tp")
    core = lax.rem(s, 2)
    chip = s // 2
    cx = lax.rem(chip, 4)
    cy = chip // 4
    sibling = s + 1 - 2 * core

    def chip_at(dy, dx):
        return lax.rem(cy + (dy + 4), 4) * 4 + lax.rem(cx + (dx + 4), 4)

    def rows(ref, start, size, step=16):
        return ref.at[pl.ds(pl.multiple_of(start, step), size)]

    def arrived(ref, sem):
        pltpu.make_async_copy(ref, ref, sem).wait()

    barrier = pltpu.get_barrier_semaphore()

    def greet_seq(i, carry):
        pl.semaphore_signal(barrier, inc=1, device_id=(lax.rem(s + i, N_SEQ), t), device_id_type=MESH)
        return carry

    def greet_tp(i, carry):
        pl.semaphore_signal(barrier, inc=1, device_id=(s, lax.rem(t + i, N_TP)), device_id_type=MESH)
        return carry

    lax.fori_loop(1, N_SEQ, greet_seq, 0)
    lax.fori_loop(1, N_TP, greet_tp, 0)

    loads = [
        pltpu.make_async_copy(source, to, load_sem.at[i])
        for i, (source, to) in enumerate(
            (
                (perm_hbm, perm), (patches_hbm, patches), (text_hbm, text), (select_hbm, select), (down_hbm, down),
                (cosine_hbm, cosine), (sine_hbm, sine), (w, w_in), (up, up_in), (mw, mwb),
            )
        )
    ]
    for load in loads:
        load.start()
    g_of = (g0, g1)

    def g_ref(c, at, blocks, phase):
        return rows(g_of[phase], (c * 16 + at) * 48, 48 * blocks)

    def g_start(phase):
        for dx, dy in ((2, 2), (1, 2), (2, 1), (3, 2), (2, 3), (1, 1), (3, 3), (1, 3), (3, 1), (2, 0), (0, 2), (1, 0), (0, 1), (3, 0), (0, 3)):
            piece = g_ref(core, chip, 1, phase)
            pltpu.make_async_remote_copy(
                src_ref=piece, dst_ref=piece, send_sem=gs_sem.at[phase], recv_sem=gr_sem.at[4 * phase + (4 - dy) % 4],
                device_id=(chip_at(dy, dx) * 2 + core, t), device_id_type=MESH,
            ).start()

    def g_row_of_chips(c, d, phase):
        return g_ref(c, lax.rem(cy + d, 4) * 4, 4, phase)

    def g_share(phase, groups):
        for d in groups:
            group = g_row_of_chips(core, d, phase)
            arrived(g_of[phase].at[pl.ds(0, 192 if d > 0 else 144)], gr_sem.at[4 * phase + d])
            pltpu.make_async_remote_copy(
                src_ref=group, dst_ref=group, send_sem=fs_sem.at[phase], recv_sem=fr_sem.at[phase],
                device_id=(sibling, t), device_id_type=MESH,
            ).start()

    def g_shared(phase, sems):
        arrived(g_of[phase].at[pl.ds(0, 768)], sems.at[phase])

    def g_sent():
        for phase in range(2):
            arrived(g_of[phase].at[pl.ds(0, 720)], gs_sem.at[phase])
            g_shared(phase, fs_sem)

    def w_start(name):
        group, total, entries = W_GROUPS[name]
        for by, bx, first, size, ty, tx, sib in entries:
            piece = rows(w_all, (chip_at(by, bx) * 2 + core) * 256 + first, size)
            pltpu.make_async_remote_copy(
                src_ref=piece, dst_ref=piece, send_sem=ws_sem.at[group], recv_sem=wr_sem.at[group],
                device_id=(sibling if sib else chip_at(ty, tx) * 2 + core, t), device_id_type=MESH,
            ).start()

    def w_wait(name):
        group, total, entries = W_GROUPS[name]
        arrived(w_all.at[pl.ds(0, total)], wr_sem.at[group])

    def w_sent():
        for group, total, entries in W_GROUPS.values():
            arrived(w_all.at[pl.ds(0, total)], ws_sem.at[group])

    right = (s, lax.rem(t + 1, N_TP))
    left = (s, lax.rem(t + N_TP - 1, N_TP))

    def ring(buf, base, size, cut, send, recv):
        def piece(origin, j):
            first = base(lax.rem(origin + 2 * N_TP, N_TP))
            return rows(buf, first + cut * j, cut if j == 0 else size - cut)

        def ways(k, j):
            return [way for way in range(2) if k < 3 or way == j]

        def start(k, j):
            for way in ways(k, j):
                part = piece(t - k if way == 0 else t + k, j)
                pltpu.make_async_remote_copy(
                    src_ref=part, dst_ref=part, send_sem=send.at[0], recv_sem=recv.at[k * 2 + j],
                    device_id=(right, left)[way], device_id_type=MESH,
                ).start()

        def wait(k, j):
            arrived(buf.at[pl.ds(0, (cut if j == 0 else size - cut) * len(ways(k, j)))], recv.at[k * 2 + j])

        def on(k, j):
            wait(k - 1, j)
            start(k, j)

        def sent():
            arrived(buf.at[pl.ds(0, 7 * size)], send.at[0])

        return start, wait, on, sent

    e_start, e_wait, e_on, e_sent = ring(tok, lambda z: z * 256 + 128, 128, 64, es_sem, er_sem)
    l_start, l_wait, l_on, l_sent = ring(tok, lambda z: z * 256, 128, 64, ls_sem, lr_sem)
    o_start, o_wait, o_on, o_sent = ring(o_all, lambda z: z * 160 + 80 * core, 80, 48, os_sem, or_sem)
    c_start, c_wait, c_on, c_sent = ring(ctx_all, lambda z: z * 160, 160, 80, cs_sem, cr_sem)

    def o_share(k):
        for origin in (t - 1 - k, t + 1 + k) if k < 3 else (t + 4,):
            piece = rows(o_all, lax.rem(origin + 2 * N_TP, N_TP) * 160 + 80 * core, 80)
            pltpu.make_async_remote_copy(
                src_ref=piece, dst_ref=piece, send_sem=ofs_sem.at[0], recv_sem=ofr_sem.at[k],
                device_id=(sibling, t), device_id_type=MESH,
            ).start()

    def o_shared(k):
        arrived(o_all.at[pl.ds(0, 160 if k < 3 else 80)], ofr_sem.at[k])

    r_640, c_640 = iota((160, 640), 0), iota((160, 640), 1)
    mine = bdot(vit_out[...], one_hot(c_640 == r_640))
    for j in range(3):
        mine += bdot(vit_qkv[j], one_hot(c_640 == r_640 + 160 * (j + 1)))
    own_g = pl.ds(pl.multiple_of((core * 16 + chip) * 48, 16), 48)
    mine = jnp.concatenate([mine, jnp.zeros((8, 640), F32)], axis=0).astype(BF16)
    g0[own_g, :] = mine[:, :256]
    g1[own_g, :] = mine[:, 256:]

    def look_up(k, carry):
        slots, len0, len1, tenant0, tenant1 = carry
        slot = slot_ref[k]
        slots = jnp.where(sessions[...] == k, slot, slots)
        at0, at1 = slot == 2 * s, slot == 2 * s + 1
        return (
            slots, jnp.where(at0, len_ref[k], len0), jnp.where(at1, len_ref[k], len1),
            jnp.where(at0, tenant_ref[k], tenant0), jnp.where(at1, tenant_ref[k], tenant1),
        )

    zero = jnp.int32(0)
    slots, len0, len1, tenant0, tenant1 = lax.fori_loop(
        0, 64, look_up, (jnp.zeros((8, 128), jnp.int32), zero, zero, zero, zero)
    )
    length = (len0, len1)

    loads[7].wait()
    own_w = pl.ds(pl.multiple_of(s * 256, 256), 256)
    for j in range(10):
        w_all[own_w, 128 * j:128 * j + 128] = w_in[j]
    loads[8].wait()
    for j in range(10):
        up_all[:, 128 * j:128 * j + 128] = up_in[j]

    pl.semaphore_wait(barrier, N_SEQ + N_TP - 2)
    g_start(0)

    own_tok = pl.multiple_of(t * 256, 256)
    loads[2].wait()
    for l in range(2):
        tok[pl.ds(own_tok + 128 + 64 * l, 64), :] = jnp.where(
            iota((64, 1024), 0) + 64 < length[l], text[128 * l + 64:128 * l + 128, :], jnp.zeros((64, 1024), BF16)
        )
    e_start(0, 0)
    e_start(0, 1)

    loads[0].wait()
    loads[1].wait()
    for n in range(5):
        lanes = slice(256 * n, 256 * n + 256)
        pp[:, lanes] = bdot(perm[...], patches[:, lanes]).astype(BF16)
    for r in range(4):
        part = slice(128 * r, 128 * r + 128)
        ln[part, :] = normalize(pp[part, :].astype(F32)).astype(BF16)

    here = (slots >> 1) == s
    folded = jnp.concatenate(
        [jnp.where(here, counts[...], 0).astype(F32), jnp.where(here, slots & 1, 0).astype(F32)], axis=0
    ).astype(BF16)
    spread = bdot(folded, one_hot((iota((128, 512), 0) >> 5) == ((iota((128, 512), 1) >> 4) & 3)))
    n_8 = iota((8, 512), 1)
    own_row = iota((8, 512), 0) == (n_8 >> 6)
    count_n = jnp.sum(jnp.where(own_row, spread[:8, :], 0.0), axis=0, keepdims=True)
    place_n = jnp.sum(jnp.where(own_row, spread[8:, :], 0.0), axis=0, keepdims=True)
    by_place = jnp.where(iota((8, 512), 0) == place_n.astype(jnp.int32), count_n, 0.0)
    n_from, n_to = iota((512, 512), 0), iota((512, 512), 1)
    before = bdot(by_place.astype(BF16), one_hot(((n_from & 15) == 0) & ((n_from >> 4) < (n_to >> 4))))
    offset_n = jnp.where(place_n > 0.5, before[1:2, :], before[0:1, :])
    visual_rows = jnp.sum(by_place, axis=1, keepdims=True) * (1.0 / 16.0)
    n_1 = n_8[0:1, :]
    row_n = jnp.where(
        (n_1 & 3).astype(F32) < count_n, place_n * 64.0 + offset_n + (n_1 & 3).astype(F32), -1.0
    ).astype(jnp.int32)

    lane_8 = iota((128, 128), 1)
    encoded_here = bdot(
        jnp.concatenate([slots.astype(F32), counts[...].astype(F32)], axis=0).astype(BF16),
        one_hot(iota((128, 128), 0) == lax.rem(s, 4) * 32 + (lane_8 >> 2)),
    )
    own_row = iota((8, 128), 0) == s // 4
    slot_c = jnp.sum(jnp.where(own_row, encoded_here[:8, :], 0.0), axis=0, keepdims=True).astype(jnp.int32)
    count_c = jnp.sum(jnp.where(own_row, encoded_here[8:, :], 0.0), axis=0, keepdims=True).astype(jnp.int32)
    target_c = (slot_c >> 1) * 16 + (lane_8[0:1, :] & 3)
    key_8 = iota((128, 128), 0)
    bias = jnp.where(((key_8 >> 2) == (lane_8 >> 2)) & ((key_8 & 3) < count_c), 0.0, -1e30)
    tenant_mask = (
        (iota((128, 256), 0) >> 4) == jnp.where((iota((128, 256), 1) & 64) == 0, tenant0, tenant1)
    ).astype(F32)

    g_share(0, (0, 1, 2, 3))
    g_start(1)
    g_shared(0, fr_sem)

    def unpack(phase):
        lanes = slice(256 * phase, 256 * phase + LANES[phase])
        for c in range(4):
            for b in range(8):
                first = ((b % 2) * 16 + 4 * c + b // 2) * 48
                wf[40 * b:40 * b + 40, lanes] = g_of[phase][first:first + 48, :].astype(F32)[:40, :]
            wall[320 * c:320 * c + 320, lanes] = wf[:, lanes].astype(BF16)

    unpack(0)
    own_o = pl.multiple_of(t * 160, 32)
    pick = one_hot(iota((160, 256), 0) == iota((160, 256), 1))
    for r in range(5):
        part = slice(256 * r, 256 * r + 256)
        o_all[pl.ds(own_o, 160), part] = bdot_nt(pick, wall[part, 0:256]).astype(BF16)
    o_start(0, 0)
    o_start(0, 1)
    e_on(1, 0)

    g_share(1, (2, 1))
    w_start("0a")
    w_start("0b")
    w_start("0s")
    g_share(1, (3, 0))
    o_on(1, 0)
    g_shared(1, fr_sem)
    unpack(1)
    o_on(1, 1)
    o_share(0)
    for n in range(2):
        lanes = slice(256 * n, 256 * n + 256)
        qkv[:, lanes] = bdot(ln[...], wall[:, 128 + 256 * n:384 + 256 * n]).astype(BF16)
    loads[3].wait()
    scale = 1.0 / math.sqrt(HEAD)
    for h in range(2):
        q_h = bdot(qkv[...], select[:, 128 * h:128 * h + 128]).astype(BF16)
        k_h = bdot(qkv[...], select[:, 256 + 128 * h:384 + 128 * h]).astype(BF16)
        v_h = bdot(qkv[...], select[:, 512 + 128 * h:640 + 128 * h])
        v_t = jnp.transpose(v_h).astype(BF16)
        for q in range(4):
            scores = bdot_nt(k_h, q_h[128 * q:128 * q + 128, :]) * scale
            scores = scores.reshape(4, 128, 128) + bias[None]
            largest = jnp.max(jnp.max(scores, axis=0), axis=0, keepdims=True)
            exponent = jnp.exp(scores - largest[None])
            total = jnp.sum(jnp.sum(exponent, axis=0), axis=0, keepdims=True)
            probs = (exponent / total[None]).astype(BF16).reshape(512, 128)
            ctx_t = bdot(v_t, probs).astype(BF16)
            ctx_all[pl.ds(own_o + 80 * h, 80), 128 * q:128 * q + 128] = ctx_t[:80, :]
        c_start(0, h)

    def project_out(z, first=False):
        at = pl.ds(pl.multiple_of(lax.rem(z + 2 * N_TP, N_TP) * 160, 32), 160)
        for n in range(5):
            lanes = slice(256 * n, 256 * n + 256)
            term = lax.dot_general(
                ctx_all[at, :], o_all[at, lanes], (((0,), (0,)), ((), ())), preferred_element_type=F32
            )
            enc[:, lanes] = (pp[:, lanes].astype(F32) if first else enc[:, lanes]) + term

    w_wait("0a")
    w_start("1a")
    o_on(2, 0)
    o_on(2, 1)
    o_share(1)
    project_out(t, True)
    c_on(1, 0)
    c_on(1, 1)
    w_wait("0b")
    w_start("1b")
    w_start("1s")
    o_shared(0)
    project_out(t - 1)
    project_out(t + 1)
    o_on(3, 0)
    o_on(3, 1)
    o_share(2)
    c_on(2, 0)
    c_on(2, 1)
    o_shared(1)
    project_out(t - 2)
    project_out(t + 2)
    o_wait(3, 0)
    o_wait(3, 1)
    o_share(3)
    c_on(3, 0)
    c_on(3, 1)
    o_shared(2)
    e_on(1, 1)
    e_on(2, 0)
    project_out(t - 3)
    project_out(t + 3)
    o_shared(3)
    loads[9].wait()
    c_wait(3, 0)
    c_wait(3, 1)
    project_out(t + 4)

    merged = jnp.zeros((128, 1024), F32)
    for j in range(4):
        merged_in = normalize(enc[128 * j:128 * j + 128, :]).astype(BF16)
        merged += bdot(merged_in, mwb[1280 * j:1280 * j + 1280, :])
    vis[...] = merged.astype(BF16)
    e_on(2, 1)

    row_512 = iota((512, 128), 0)
    outgoing = jnp.zeros((512, 256), F32)
    for q in range(4):
        outgoing += bdot(one_hot(row_512 == target_c + 4 * q), vis[:, 256 * q:256 * q + 256])
    xs[...] = outgoing.astype(BF16)

    def send_rows(i, carry):
        to = lax.rem(s + i, N_SEQ)
        pltpu.make_async_remote_copy(
            src_ref=rows(xs, to * 16, 16), dst_ref=rows(ys, s * 16, 16),
            send_sem=as_sem.at[0], recv_sem=ar_sem.at[0], device_id=(to, t), device_id_type=MESH,
        ).start()
        return carry

    lax.fori_loop(1, N_SEQ, send_rows, 0)
    own_y = pl.ds(pl.multiple_of(s * 16, 16), 16)
    ys[own_y, :] = xs[own_y, :]
    e_on(3, 0)
    e_on(3, 1)
    arrived(ys.at[pl.ds(0, 496)], ar_sem.at[0])
    w_wait("1a")
    w_start("2a")
    w_wait("1b")
    w_start("2b")
    w_start("2s")

    row_128 = iota((128, 512), 0)
    position = iota((64, 256), 0)
    for q in range(4):
        lanes = slice(256 * q, 256 * q + 256)
        picked = bdot(one_hot((row_128 == row_n) & (((n_1 >> 2) & 3) == q)), ys[...]).astype(BF16)
        for l in range(2):
            is_text = (position.astype(F32) >= visual_rows[l:l + 1, :]) & (position < length[l])
            tok[pl.ds(own_tok + 64 * l, 64), lanes] = jnp.where(
                is_text, text[128 * l:128 * l + 64, lanes], picked[64 * l:64 * l + 64, :]
            )
    l_start(0, 0)
    l_start(0, 1)

    loads[4].wait()
    down_sums = jnp.transpose(bdot(tok[pl.ds(own_tok, 256), :], down[...])) * tenant_mask
    dl[pl.ds(pl.multiple_of(t * 16, 16), 16), :] = jnp.sum(down_sums.reshape(8, 16, 256), axis=0)

    def send_down(i, carry):
        piece = rows(dl, t * 16, 16)
        pltpu.make_async_remote_copy(
            src_ref=piece, dst_ref=piece, send_sem=ds_sem.at[0], recv_sem=dr_sem.at[0],
            device_id=(s, lax.rem(t + i, N_TP)), device_id_type=MESH,
        ).start()
        return carry

    lax.fori_loop(1, N_TP, send_down, 0)

    def project(far, nearest, farthest):
        for z in range(8):
            distance = min(z, N_TP - z)
            if not nearest <= distance <= farthest:
                continue
            z = lax.rem(t + z, N_TP)
            x = tok[pl.ds(pl.multiple_of(z * 256, 256), 256), :]
            first = pl.multiple_of(z * 1024, 1024)
            for n in range(5):
                lanes = slice(256 * n, 256 * n + 256)
                acc[:, lanes] += bdot(x, w_all[pl.ds(first, 1024), lanes])
            x_wide = x.astype(F32)
            x_wide = x_wide * x_wide
            for n in range(8):
                squares[...] += x_wide[:, 128 * n:128 * n + 128]

    acc[...] = jnp.zeros_like(acc)
    squares[...] = jnp.zeros_like(squares)
    l_on(1, 0)
    l_on(1, 1)
    for name in ("0s", "1s", "2s"):
        w_wait(name)
    l_on(2, 0)
    w_wait("2a")
    w_start("3a")
    w_wait("2b")
    w_start("3b")
    w_start("3s")
    l_on(2, 1)
    e_wait(3, 0)
    e_wait(3, 1)
    w_wait("3a")
    w_wait("3b")
    w_start("4s")
    l_on(3, 0)
    l_on(3, 1)
    w_wait("3s")
    w_wait("4s")
    project(True, 0, 3)
    arrived(dl.at[pl.ds(0, 112)], dr_sem.at[0])
    down_t = jnp.sum(dl[...].reshape(8, 16, 256), axis=0)
    lora = jnp.transpose(jnp.concatenate([down_t] * 8, axis=0) * tenant_mask).astype(BF16)
    acc[...] += bdot(lora, up_all[...])
    l_wait(3, 0)
    l_wait(3, 1)
    project(None, 4, 4)
    inverse = lax.rsqrt(jnp.sum(squares[...], axis=1, keepdims=True) * (1.0 / DECODER_WIDTH) + EPSILON)

    loads[5].wait()
    loads[6].wait()

    causal = iota((128, 128), 0) >= iota((128, 128), 1)
    ones = jnp.ones((128, 128), BF16)
    stores = []
    for l in range(2):
        low, high = slice(64 * l, 64 * l + 64), slice(128 + 64 * l, 192 + 64 * l)
        factor = jnp.concatenate([inverse[low, :], inverse[high, :]], axis=0)

        def column(index):
            lanes = slice(128 * index, 128 * index + 128)
            return jnp.concatenate([acc[low, lanes], acc[high, lanes]], axis=0) * factor

        def rotate(values):
            return values * cosine[...] + pltpu.roll(values, 64, 1) * sine[...]

        key_rows = rotate(column(8)).astype(BF16)
        value_rows = jnp.concatenate([column(9).astype(BF16), ones], axis=1)
        kept = iota((128, 128), 0) < length[l]
        for j in range(QUERY_PER_KEY):
            query = rotate(column(j)).astype(BF16)
            scores = bdot_nt(query, key_rows) * (1.0 / math.sqrt(DECODER_HEAD_DIM))
            scores = jnp.where(causal, scores, -1e30)
            exponent = jnp.exp(scores - jnp.max(scores, axis=1, keepdims=True)).astype(BF16)
            summed = bdot(exponent, value_rows)
            res[128 * l:128 * l + 128, 128 * j:128 * j + 128] = jnp.where(
                kept, summed[:, :128] / summed[:, 128:], 0.0
            ).astype(BF16)
        stores.append(pltpu.make_async_copy(
            res.at[pl.ds(128 * l, 128)], out.at[pl.ds(128 * l, 128)], load_sem.at[10 + l]
        ))
        stores[l].start()

    for store in stores:
        store.wait()
    g_sent()
    w_sent()
    e_sent()
    l_sent()
    o_sent()
    c_sent()
    arrived(o_all.at[pl.ds(0, 560)], ofs_sem.at[0])
    arrived(xs.at[pl.ds(0, 496)], as_sem.at[0])
    arrived(dl.at[pl.ds(0, 112)], ds_sem.at[0])


def on_device(
    patches, vit_qkv, vit_out, merge_weight, query_key_value_weight, adapter_down, adapter_up_weight,
    text_embed, vis_count, image_session, session_slot, session_tenant, session_len,
):
    operands = (
        session_slot, session_tenant, session_len, vis_count.reshape(8, 128), image_session.reshape(8, 128),
        vit_qkv, vit_out.T, patches.reshape(512, DV), merge_weight,
        jnp.transpose(query_key_value_weight.reshape(256, 10, 128), (1, 0, 2)), adapter_down,
        jnp.transpose(adapter_up_weight.reshape(128, 10, 128), (1, 0, 2)), text_embed,
    ) + tables()
    vmem = pl.BlockSpec(memory_space=pltpu.VMEM)
    smem = pl.BlockSpec(memory_space=pltpu.SMEM)
    hbm = pl.BlockSpec(memory_space=pl.ANY)
    dma = pltpu.SemaphoreType.DMA
    return pl.pallas_call(
        kernel,
        out_shape=jax.ShapeDtypeStruct((256, 1024), BF16),
        in_specs=[smem if i < 3 else vmem if i < 7 else hbm for i in range(len(operands))],
        out_specs=hbm,
        scratch_shapes=[
            pltpu.VMEM((512, 1280), BF16),
            pltpu.VMEM((1024, 128), BF16),
            pltpu.VMEM((256, 1024), BF16),
            pltpu.VMEM((512, 512), BF16),
            pltpu.VMEM((512, 768), BF16),
            pltpu.VMEM((128, 128), F32),
            pltpu.VMEM((128, 128), F32),
            pltpu.VMEM((10, 256, 128), BF16),
            pltpu.VMEM((10, 128, 128), BF16),
            pltpu.VMEM((1536, LANES[0]), BF16),
            pltpu.VMEM((1536, LANES[1]), BF16),
            pltpu.VMEM((320, 640), F32),
            pltpu.VMEM((1280, 640), BF16),
            pltpu.VMEM((512, 1280), BF16),
            pltpu.VMEM((512, 1280), BF16),
            pltpu.VMEM((512, 512), BF16),
            pltpu.VMEM((1280, 1280), BF16),
            pltpu.VMEM((1280, 512), BF16),
            pltpu.VMEM((512, 1280), F32),
            pltpu.VMEM((5120, 1024), BF16),
            pltpu.VMEM((128, 1024), BF16),
            pltpu.VMEM((512, 256), BF16),
            pltpu.VMEM((512, 256), BF16),
            pltpu.VMEM((2048, 1024), BF16),
            pltpu.VMEM((128, 256), F32),
            pltpu.VMEM((8192, 1280), BF16),
            pltpu.VMEM((128, 1280), BF16),
            pltpu.VMEM((256, 1280), F32),
            pltpu.VMEM((256, 128), F32),
            pltpu.VMEM((256, 1024), BF16),
            dma((12,)), dma((2,)), dma((8,)), dma((2,)), dma((2,)), dma((len(W_GROUPS),)), dma((len(W_GROUPS),)),
            dma((1,)), dma((8,)), dma((1,)), dma((4,)),
            dma((1,)), dma((8,)), dma((1,)), dma((8,)), dma((1,)), dma((8,)),
            dma((1,)), dma((1,)), dma((1,)), dma((1,)),
        ],
        compiler_params=pltpu.CompilerParams(
            collective_id=0, has_side_effects=True, vmem_limit_bytes=64 * 1024 * 1024
        ),
    )(*operands).astype(F32)


def solution(mesh):
    placed = (
        P("seq", None, None),
        P(None, "seq", "tp"),
        P("tp", "seq"),
        P(None, "tp"),
        P("seq", "tp", None, None),
        P("tp", None),
        P(None, "tp", None, None),
        P("seq", "tp"),
        P(),
        P(),
        P(),
        P(),
        P(),
    )
    return jax.shard_map(
        on_device, mesh=mesh, in_specs=placed, out_specs=P("seq", "tp"), check_vma=False
    )
```

time: 122 us -> 111 us (0.910)
  local copies, waits for them, and re-layouts: 8.3 us -> 0 us
  Pallas kernels: 113 us -> 108 us
  other arithmetic: 0 us -> 2.13 us
    unnamed x4 -> x0, local copies, waits for them, and re-layouts: 8.3 us -> none
    pallas_call x1, Pallas kernels: 113 us -> 108 us  [on_device(): pl.pallas_call(kernel, out_shape=jax.ShapeDtypeStruct((256, 1024), BF16),...]
    convert_element_type x0 -> x1, other arithmetic: none -> 2.13 us  [on_device(): return pl.pallas_call(kernel, out_shape=jax.ShapeDtypeStruct((256, 1024),...]
where the time goes in v3:
time: 111 us
  Pallas kernels  108 us (97%)
  other arithmetic  2.13 us (2%)
    pallas_call x1, Pallas kernels, on_device(): pl.pallas_call(kernel, out_shape=jax.ShapeDtypeStruct((256, 1024), BF16),...  108 us

profile of v3, /device:TPU:1, one launch (start us, length us, event | category | flops | bytes accessed | tf_op | source)
XLA Modules:
  0.0 110.6 jit_solution(5448205630283277356)
XLA Ops:
  0.0 108.4 %shard_map.163 = bf16[256,1024]{1,0:T(8,128)(2,1)} custom-call(s32[64]{0:T(128)} %slot_ref.1, s32[64]{0:T(128)} %tenant_ref.1, s32[64]{0:T(128)} %len_ref.1, s32[8,128]{1,0:T(8,128)} %bitcast.14, s32[8,128]{1,0:T(8,128)} %bitcast.15, bf16[3,40,160]{2,1,0:T(8,128)(2,1)} %vit_qkv.1, bf16[40,160]{1,0:T(8,128)(2,1)} %bitcast.13, bf16[512,1280]{1,0:T(8,128)(2,1)} %bitcast.10, ...), custom_call_target="tpu_custom_call" | custom-call | tf_op jit(solution)/shard_map/pallas_call | solution.py:622
  108.4 2.1 %convert_element_type.3 = f32[256,1024]{1,0:T(8,128)} convert(bf16[256,1024]{1,0:T(8,128)(2,1)} %shard_map.163) | non-fusion elementwise | flops 262144 | bytes 1572864 | tf_op jit(solution)/shard_map/convert_element_type | solution.py:666

commit v4 on v3

--- a/solution.py
+++ b/solution.py
@@ -71,16 +71,17 @@
         "0s": sib([(0, 0)]),
         "1a": [go(0, -1, part_a, 0, 1), go(-1, 0, part_a, 1, 0)]
         + [go(0, side, part_a, to, 0) for side in sides for to in sides],
-        "1b": [go(0, 1, part_b, 0, -1), go(1, 0, part_b, -1, 0)]
+        "1b": [go(1, 0, part_b, -1, 0)]
         + [go(side, 0, part_b, 0, to) for side in sides for to in sides],
+        "1c": [go(0, 1, (128, 64), 0, -1), go(0, -1, (192, 64), 0, 1)],
         "1s": sib(near),
         "2a": [go(0, 2, part_a, 1, 0), go(0, 2, part_a, -1, 0), go(-1, 1, part_a, 1, 0), go(1, -1, part_a, -1, 0)],
         "2b": [go(2, 0, part_b, 0, 1), go(2, 0, part_b, 0, -1), go(1, -1, part_b, 0, 1), go(-1, 1, part_b, 0, -1)],
-        "2s": sib([(0, 2), (2, 0), (-1, -1), (-1, 1), (1, -1), (1, 1)]),
+        "2s": sib([(2, 0), (-1, -1), (-1, 1), (1, -1), (1, 1)]),
         "3a": [go(-1, 2, (0, 64), 1, 0), go(1, 2, (64, 64), -1, 0)],
         "3b": [go(2, -1, (128, 64), 0, 1), go(2, 1, (192, 64), 0, -1)],
         "3s": sib([(-1, 2), (1, 2), (2, -1), (2, 1)]),
-        "4s": sib([(2, 2)]),
+        "4s": sib([(0, 2), (2, 2)]),
     }
     return {
         name: (i, sum(entry[3] for entry in entries), entries) for i, (name, entries) in enumerate(lists.items())
@@ -218,24 +219,27 @@
     right = (s, lax.rem(t + 1, N_TP))
     left = (s, lax.rem(t + N_TP - 1, N_TP))
 
-    def ring(buf, base, size, cut, send, recv):
+    def ring(buf, base, size, cut, send, recv, crossed):
         def piece(origin, j):
             first = base(lax.rem(origin + 2 * N_TP, N_TP))
             return rows(buf, first + cut * j, cut if j == 0 else size - cut)
 
         def ways(k, j):
-            return [way for way in range(2) if k < 3 or way == j]
+            both = [(0, j), (1, 1 - j if crossed else j)]
+            return both if k < 3 else [(way, part) for way, part in both if part == way]
 
         def start(k, j):
-            for way in ways(k, j):
-                part = piece(t - k if way == 0 else t + k, j)
+            for way, part in ways(k, j):
+                block = piece(t - k if way == 0 else t + k, part)
                 pltpu.make_async_remote_copy(
-                    src_ref=part, dst_ref=part, send_sem=send.at[0], recv_sem=recv.at[k * 2 + j],
+                    src_ref=block, dst_ref=block, send_sem=send.at[0], recv_sem=recv.at[k * 2 + j],
                     device_id=(right, left)[way], device_id_type=MESH,
                 ).start()
 
         def wait(k, j):
-            arrived(buf.at[pl.ds(0, (cut if j == 0 else size - cut) * len(ways(k, j)))], recv.at[k * 2 + j])
+            total = sum((cut, size - cut)[part] for way, part in ways(k, j))
+            if total > 0:
+                arrived(buf.at[pl.ds(0, total)], recv.at[k * 2 + j])
 
         def on(k, j):
             wait(k - 1, j)
@@ -246,10 +250,10 @@
 
         return start, wait, on, sent
 
-    e_start, e_wait, e_on, e_sent = ring(tok, lambda z: z * 256 + 128, 128, 64, es_sem, er_sem)
-    l_start, l_wait, l_on, l_sent = ring(tok, lambda z: z * 256, 128, 64, ls_sem, lr_sem)
-    o_start, o_wait, o_on, o_sent = ring(o_all, lambda z: z * 160 + 80 * core, 80, 48, os_sem, or_sem)
-    c_start, c_wait, c_on, c_sent = ring(ctx_all, lambda z: z * 160, 160, 80, cs_sem, cr_sem)
+    e_start, e_wait, e_on, e_sent = ring(tok, lambda z: z * 256 + 128, 128, 64, es_sem, er_sem, True)
+    l_start, l_wait, l_on, l_sent = ring(tok, lambda z: z * 256, 128, 64, ls_sem, lr_sem, True)
+    o_start, o_wait, o_on, o_sent = ring(o_all, lambda z: z * 160 + 80 * core, 80, 48, os_sem, or_sem, True)
+    c_start, c_wait, c_on, c_sent = ring(ctx_all, lambda z: z * 160, 160, 80, cs_sem, cr_sem, True)
 
     def o_share(k):
         for origin in (t - 1 - k, t + 1 + k) if k < 3 else (t + 4,):
@@ -350,7 +354,7 @@
         (iota((128, 256), 0) >> 4) == jnp.where((iota((128, 256), 1) & 64) == 0, tenant0, tenant1)
     ).astype(F32)
 
-    g_share(0, (0, 1, 2, 3))
+    g_share(0, (2, 3, 1, 0))
     g_start(1)
     g_shared(0, fr_sem)
 
@@ -370,13 +374,12 @@
         o_all[pl.ds(own_o, 160), part] = bdot_nt(pick, wall[part, 0:256]).astype(BF16)
     o_start(0, 0)
     o_start(0, 1)
-    e_on(1, 0)
-
-    g_share(1, (2, 1))
+
+    g_share(1, (2, 3))
     w_start("0a")
     w_start("0b")
     w_start("0s")
-    g_share(1, (3, 0))
+    g_share(1, (1, 0))
     o_on(1, 0)
     g_shared(1, fr_sem)
     unpack(1)
@@ -401,7 +404,9 @@
             probs = (exponent / total[None]).astype(BF16).reshape(512, 128)
             ctx_t = bdot(v_t, probs).astype(BF16)
             ctx_all[pl.ds(own_o + 80 * h, 80), 128 * q:128 * q + 128] = ctx_t[:80, :]
-        c_start(0, h)
+
+    c_start(0, 0)
+    c_start(0, 1)
 
     def project_out(z, first=False):
         at = pl.ds(pl.multiple_of(lax.rem(z + 2 * N_TP, N_TP) * 160, 32), 160)
@@ -412,17 +417,14 @@
             )
             enc[:, lanes] = (pp[:, lanes].astype(F32) if first else enc[:, lanes]) + term
 
-    w_wait("0a")
-    w_start("1a")
     o_on(2, 0)
     o_on(2, 1)
     o_share(1)
     project_out(t, True)
     c_on(1, 0)
     c_on(1, 1)
-    w_wait("0b")
-    w_start("1b")
-    w_start("1s")
+    w_wait("0a")
+    w_start("1a")
     o_shared(0)
     project_out(t - 1)
     project_out(t + 1)
@@ -431,23 +433,24 @@
     o_share(2)
     c_on(2, 0)
     c_on(2, 1)
+    w_wait("0b")
+    w_start("1b")
+    w_start("1s")
     o_shared(1)
     project_out(t - 2)
     project_out(t + 2)
     o_wait(3, 0)
-    o_wait(3, 1)
     o_share(3)
     c_on(3, 0)
     c_on(3, 1)
     o_shared(2)
+    e_on(1, 0)
     e_on(1, 1)
-    e_on(2, 0)
     project_out(t - 3)
     project_out(t + 3)
     o_shared(3)
     loads[9].wait()
     c_wait(3, 0)
-    c_wait(3, 1)
     project_out(t + 4)
 
     merged = jnp.zeros((128, 1024), F32)
@@ -455,7 +458,7 @@
         merged_in = normalize(enc[128 * j:128 * j + 128, :]).astype(BF16)
         merged += bdot(merged_in, mwb[1280 * j:1280 * j + 1280, :])
     vis[...] = merged.astype(BF16)
-    e_on(2, 1)
+    e_on(2, 0)
 
     row_512 = iota((512, 128), 0)
     outgoing = jnp.zeros((512, 256), F32)
@@ -474,14 +477,11 @@
     lax.fori_loop(1, N_SEQ, send_rows, 0)
     own_y = pl.ds(pl.multiple_of(s * 16, 16), 16)
     ys[own_y, :] = xs[own_y, :]
-    e_on(3, 0)
-    e_on(3, 1)
-    arrived(ys.at[pl.ds(0, 496)], ar_sem.at[0])
+    e_on(2, 1)
     w_wait("1a")
     w_start("2a")
-    w_wait("1b")
-    w_start("2b")
-    w_start("2s")
+    e_on(3, 0)
+    arrived(ys.at[pl.ds(0, 496)], ar_sem.at[0])
 
     row_128 = iota((128, 512), 0)
     position = iota((64, 256), 0)
@@ -495,6 +495,10 @@
             )
     l_start(0, 0)
     l_start(0, 1)
+    w_wait("1b")
+    w_start("2b")
+    w_start("1c")
+    w_start("2s")
 
     loads[4].wait()
     down_sums = jnp.transpose(bdot(tok[pl.ds(own_tok, 256), :], down[...])) * tenant_mask
@@ -510,52 +514,66 @@
 
     lax.fori_loop(1, N_TP, send_down, 0)
 
-    def project(far, nearest, farthest):
-        for z in range(8):
-            distance = min(z, N_TP - z)
-            if not nearest <= distance <= farthest:
-                continue
-            z = lax.rem(t + z, N_TP)
-            x = tok[pl.ds(pl.multiple_of(z * 256, 256), 256), :]
-            first = pl.multiple_of(z * 1024, 1024)
+    near = [(0, 0), (0, -1), (0, 1), (-1, 0), (1, 0), (2, 0), (-1, -1), (-1, 1), (1, -1), (1, 1)]
+    far = [(-1, 2), (1, 2), (2, -1), (2, 1), (0, 2), (2, 2)]
+
+    def project(chips, top, size):
+        for by, bx in chips:
+            at = chip_at(by, bx)
+            odd = lax.rem(at, 2)
+            even = (1 - odd).astype(F32).astype(BF16)
+            odd = odd.astype(F32).astype(BF16)
+            of_z = pl.ds(pl.multiple_of(at // 2 * 256 + top, 128), size)
+            x = tok[of_z, 0:512] * even + tok[of_z, 512:1024] * odd
+            first = pl.multiple_of(at * 512, 512)
             for n in range(5):
                 lanes = slice(256 * n, 256 * n + 256)
-                acc[:, lanes] += bdot(x, w_all[pl.ds(first, 1024), lanes])
-            x_wide = x.astype(F32)
-            x_wide = x_wide * x_wide
+                acc[top:top + size, lanes] += bdot(x, w_all[pl.ds(first, 512), lanes])
+
+    def add_squares(aheads, top):
+        for ahead in aheads:
+            of_z = pl.ds(pl.multiple_of(lax.rem(t + ahead + N_TP, N_TP) * 256 + top, 128), 128)
+            total = squares[top:top + 128, :]
             for n in range(8):
-                squares[...] += x_wide[:, 128 * n:128 * n + 128]
+                part = tok[of_z, 128 * n:128 * n + 128].astype(F32)
+                total += part * part
+            squares[top:top + 128, :] = total
 
     acc[...] = jnp.zeros_like(acc)
     squares[...] = jnp.zeros_like(squares)
     l_on(1, 0)
+    e_wait(2, 1)
+    e_wait(3, 0)
+    add_squares(range(8), 128)
     l_on(1, 1)
-    for name in ("0s", "1s", "2s"):
+    add_squares((0, 1, -1), 0)
+    for name in ("0s", "1s"):
         w_wait(name)
     l_on(2, 0)
+    w_wait("2s")
+    l_on(2, 1)
     w_wait("2a")
     w_start("3a")
+    add_squares((2, -2), 0)
+    l_on(3, 0)
     w_wait("2b")
     w_start("3b")
     w_start("3s")
-    l_on(2, 1)
-    e_wait(3, 0)
-    e_wait(3, 1)
-    w_wait("3a")
-    w_wait("3b")
+    l_on(3, 1)
+    add_squares((3, -3), 0)
+    for name in ("1c", "3a", "3b"):
+        w_wait(name)
     w_start("4s")
-    l_on(3, 0)
-    l_on(3, 1)
-    w_wait("3s")
-    w_wait("4s")
-    project(True, 0, 3)
     arrived(dl.at[pl.ds(0, 112)], dr_sem.at[0])
     down_t = jnp.sum(dl[...].reshape(8, 16, 256), axis=0)
     lora = jnp.transpose(jnp.concatenate([down_t] * 8, axis=0) * tenant_mask).astype(BF16)
     acc[...] += bdot(lora, up_all[...])
     l_wait(3, 0)
-    l_wait(3, 1)
-    project(None, 4, 4)
+    add_squares((4,), 0)
+    w_wait("3s")
+    w_wait("4s")
+    project(near, 0, 256)
+    project(far, 0, 256)
     inverse = lax.rsqrt(jnp.sum(squares[...], axis=1, keepdims=True) * (1.0 / DECODER_WIDTH) + EPSILON)
 
     loads[5].wait()

time: 111 us -> 117 us (1.054)
  Pallas kernels: 108 us -> 114 us
    pallas_call x1, Pallas kernels: 108 us -> 114 us  [on_device(): pl.pallas_call(kernel, out_shape=jax.ShapeDtypeStruct((256, 1024), BF16),...]
where the time goes in v4:
time: 117 us; the launch traced here: 116 us
  Pallas kernels  114 us (97%)
  other arithmetic  2.13 us (2%)
    pallas_call x1, Pallas kernels, on_device(): pl.pallas_call(kernel, out_shape=jax.ShapeDtypeStruct((256, 1024), BF16),...  114 us

profile of v4, /device:TPU:1, one launch (start us, length us, event | category | flops | bytes accessed | tf_op | source)
XLA Modules:
  0.0 116.4 jit_solution(10790989107044419001)
XLA Ops:
  0.0 114.2 %shard_map.163 = bf16[256,1024]{1,0:T(8,128)(2,1)} custom-call(s32[64]{0:T(128)} %slot_ref.1, s32[64]{0:T(128)} %tenant_ref.1, s32[64]{0:T(128)} %len_ref.1, s32[8,128]{1,0:T(8,128)} %bitcast.14, s32[8,128]{1,0:T(8,128)} %bitcast.15, bf16[3,40,160]{2,1,0:T(8,128)(2,1)} %vit_qkv.1, bf16[40,160]{1,0:T(8,128)(2,1)} %bitcast.13, bf16[512,1280]{1,0:T(8,128)(2,1)} %bitcast.10, ...), custom_call_target="tpu_custom_call" | custom-call | tf_op jit(solution)/shard_map/pallas_call | solution.py:640
  114.3 2.1 %convert_element_type.3 = f32[256,1024]{1,0:T(8,128)} convert(bf16[256,1024]{1,0:T(8,128)(2,1)} %shard_map.163) | non-fusion elementwise | flops 262144 | bytes 1572864 | tf_op jit(solution)/shard_map/convert_element_type | solution.py:684

commit v5 on v4

--- a/solution.py
+++ b/solution.py
@@ -89,6 +89,8 @@
 
 
 W_GROUPS = plane_copies()
+NEAR = [(0, 0), (0, 3), (0, 1), (3, 0), (1, 0), (2, 0), (3, 3), (3, 1), (1, 3), (1, 1)]
+FAR = [(3, 2), (1, 2), (2, 3), (2, 1), (0, 2), (2, 2)]
 LANES = (256, 384)
 
 
@@ -120,7 +122,7 @@
     patches_hbm, mw, w, down_hbm, up, text_hbm, perm_hbm, select_hbm, cosine_hbm, sine_hbm,
     out,
     patches, down, text, perm, select, cosine, sine, w_in, up_in,
-    g0, g1, wf, wall, pp, ln, qkv, o_all, ctx_all, enc, mwb, vis, xs, ys, tok, dl, w_all, up_all, acc, squares, res,
+    g0, g1, wf, wall, pp, ln, qkv, o_all, ctx_all, enc, mwb, vis, xs, ys, tok_l, tok_e, dl, w_near, w_far, up_all, acc, squares, res,
     load_sem, gs_sem, gr_sem, fs_sem, fr_sem, ws_sem, wr_sem,
     os_sem, or_sem, ofs_sem, ofr_sem, cs_sem, cr_sem, es_sem, er_sem, ls_sem, lr_sem,
     as_sem, ar_sem, ds_sem, dr_sem,
@@ -199,22 +201,27 @@
             arrived(g_of[phase].at[pl.ds(0, 720)], gs_sem.at[phase])
             g_shared(phase, fs_sem)
 
+    def w_ref(c, by, bx, first, size):
+        place = (by % 4, bx % 4)
+        buf, order = (w_near, NEAR) if place in NEAR else (w_far, FAR)
+        return rows(buf, order.index(place) * 512 + c * 256 + first, size)
+
     def w_start(name):
         group, total, entries = W_GROUPS[name]
         for by, bx, first, size, ty, tx, sib in entries:
-            piece = rows(w_all, (chip_at(by, bx) * 2 + core) * 256 + first, size)
             pltpu.make_async_remote_copy(
-                src_ref=piece, dst_ref=piece, send_sem=ws_sem.at[group], recv_sem=wr_sem.at[group],
+                src_ref=w_ref(core, by, bx, first, size), dst_ref=w_ref(core, by - ty, bx - tx, first, size),
+                send_sem=ws_sem.at[group], recv_sem=wr_sem.at[group],
                 device_id=(sibling if sib else chip_at(ty, tx) * 2 + core, t), device_id_type=MESH,
             ).start()
 
     def w_wait(name):
         group, total, entries = W_GROUPS[name]
-        arrived(w_all.at[pl.ds(0, total)], wr_sem.at[group])
+        arrived(w_near.at[pl.ds(0, total)], wr_sem.at[group])
 
     def w_sent():
         for group, total, entries in W_GROUPS.values():
-            arrived(w_all.at[pl.ds(0, total)], ws_sem.at[group])
+            arrived(w_near.at[pl.ds(0, total)], ws_sem.at[group])
 
     right = (s, lax.rem(t + 1, N_TP))
     left = (s, lax.rem(t + N_TP - 1, N_TP))
@@ -250,8 +257,8 @@
 
         return start, wait, on, sent
 
-    e_start, e_wait, e_on, e_sent = ring(tok, lambda z: z * 256 + 128, 128, 64, es_sem, er_sem, True)
-    l_start, l_wait, l_on, l_sent = ring(tok, lambda z: z * 256, 128, 64, ls_sem, lr_sem, True)
+    e_start, e_wait, e_on, e_sent = ring(tok_e, lambda z: z * 128, 128, 64, es_sem, er_sem, True)
+    l_start, l_wait, l_on, l_sent = ring(tok_l, lambda z: z * 128, 128, 64, ls_sem, lr_sem, True)
     o_start, o_wait, o_on, o_sent = ring(o_all, lambda z: z * 160 + 80 * core, 80, 48, os_sem, or_sem, True)
     c_start, c_wait, c_on, c_sent = ring(ctx_all, lambda z: z * 160, 160, 80, cs_sem, cr_sem, True)
 
@@ -292,9 +299,9 @@
     length = (len0, len1)
 
     loads[7].wait()
-    own_w = pl.ds(pl.multiple_of(s * 256, 256), 256)
+    own_w = pl.ds(pl.multiple_of(core * 256, 256), 256)
     for j in range(10):
-        w_all[own_w, 128 * j:128 * j + 128] = w_in[j]
+        w_near[own_w, 128 * j:128 * j + 128] = w_in[j]
     loads[8].wait()
     for j in range(10):
         up_all[:, 128 * j:128 * j + 128] = up_in[j]
@@ -302,10 +309,10 @@
     pl.semaphore_wait(barrier, N_SEQ + N_TP - 2)
     g_start(0)
 
-    own_tok = pl.multiple_of(t * 256, 256)
+    own_tok = pl.multiple_of(t * 128, 128)
     loads[2].wait()
     for l in range(2):
-        tok[pl.ds(own_tok + 128 + 64 * l, 64), :] = jnp.where(
+        tok_e[pl.ds(own_tok + 64 * l, 64), :] = jnp.where(
             iota((64, 1024), 0) + 64 < length[l], text[128 * l + 64:128 * l + 128, :], jnp.zeros((64, 1024), BF16)
         )
     e_start(0, 0)
@@ -490,7 +497,7 @@
         picked = bdot(one_hot((row_128 == row_n) & (((n_1 >> 2) & 3) == q)), ys[...]).astype(BF16)
         for l in range(2):
             is_text = (position.astype(F32) >= visual_rows[l:l + 1, :]) & (position < length[l])
-            tok[pl.ds(own_tok + 64 * l, 64), lanes] = jnp.where(
+            tok_l[pl.ds(own_tok + 64 * l, 64), lanes] = jnp.where(
                 is_text, text[128 * l:128 * l + 64, lanes], picked[64 * l:64 * l + 64, :]
             )
     l_start(0, 0)
@@ -501,7 +508,8 @@
     w_start("2s")
 
     loads[4].wait()
-    down_sums = jnp.transpose(bdot(tok[pl.ds(own_tok, 256), :], down[...])) * tenant_mask
+    own_rows = jnp.concatenate([tok_l[pl.ds(own_tok, 128), :], tok_e[pl.ds(own_tok, 128), :]], axis=0)
+    down_sums = jnp.transpose(bdot(own_rows, down[...])) * tenant_mask
     dl[pl.ds(pl.multiple_of(t * 16, 16), 16), :] = jnp.sum(down_sums.reshape(8, 16, 256), axis=0)
 
     def send_down(i, carry):
@@ -514,25 +522,27 @@
 
     lax.fori_loop(1, N_TP, send_down, 0)
 
-    near = [(0, 0), (0, -1), (0, 1), (-1, 0), (1, 0), (2, 0), (-1, -1), (-1, 1), (1, -1), (1, 1)]
-    far = [(-1, 2), (1, 2), (2, -1), (2, 1), (0, 2), (2, 2)]
-
-    def project(chips, top, size):
+    def project(chips, late, early):
+        tops = [top for top, due in ((0, late), (128, early)) if due]
+        buf, order = (w_near, NEAR) if chips[0] in NEAR else (w_far, FAR)
         for by, bx in chips:
             at = chip_at(by, bx)
             odd = lax.rem(at, 2)
             even = (1 - odd).astype(F32).astype(BF16)
             odd = odd.astype(F32).astype(BF16)
-            of_z = pl.ds(pl.multiple_of(at // 2 * 256 + top, 128), size)
-            x = tok[of_z, 0:512] * even + tok[of_z, 512:1024] * odd
-            first = pl.multiple_of(at * 512, 512)
+            of_z = pl.ds(pl.multiple_of(at // 2 * 128, 128), 128)
+            parts = [(tok_l, tok_e)[top // 128] for top in tops]
+            parts = [part[of_z, 0:512] * even + part[of_z, 512:1024] * odd for part in parts]
+            x = jnp.concatenate(parts, axis=0) if len(parts) > 1 else parts[0]
+            rows_of = slice(tops[0], tops[-1] + 128)
+            first = order.index((by, bx)) * 512
             for n in range(5):
                 lanes = slice(256 * n, 256 * n + 256)
-                acc[top:top + size, lanes] += bdot(x, w_all[pl.ds(first, 512), lanes])
-
-    def add_squares(aheads, top):
+                acc[rows_of, lanes] += bdot(x, buf[first:first + 512, lanes])
+
+    def add_squares(aheads, tok, top):
         for ahead in aheads:
-            of_z = pl.ds(pl.multiple_of(lax.rem(t + ahead + N_TP, N_TP) * 256 + top, 128), 128)
+            of_z = pl.ds(pl.multiple_of(lax.rem(t + ahead + N_TP, N_TP) * 128, 128), 128)
             total = squares[top:top + 128, :]
             for n in range(8):
                 part = tok[of_z, 128 * n:128 * n + 128].astype(F32)
@@ -544,23 +554,25 @@
     l_on(1, 0)
     e_wait(2, 1)
     e_wait(3, 0)
-    add_squares(range(8), 128)
+    add_squares(range(8), tok_e, 128)
     l_on(1, 1)
-    add_squares((0, 1, -1), 0)
+    add_squares((0, 1, -1), tok_l, 0)
     for name in ("0s", "1s"):
         w_wait(name)
+    project(NEAR[:5], False, True)
     l_on(2, 0)
     w_wait("2s")
+    project(NEAR[5:], False, True)
     l_on(2, 1)
     w_wait("2a")
     w_start("3a")
-    add_squares((2, -2), 0)
+    add_squares((2, -2), tok_l, 0)
     l_on(3, 0)
     w_wait("2b")
     w_start("3b")
     w_start("3s")
     l_on(3, 1)
-    add_squares((3, -3), 0)
+    add_squares((3, -3), tok_l, 0)
     for name in ("1c", "3a", "3b"):
         w_wait(name)
     w_start("4s")
@@ -569,11 +581,11 @@
     lora = jnp.transpose(jnp.concatenate([down_t] * 8, axis=0) * tenant_mask).astype(BF16)
     acc[...] += bdot(lora, up_all[...])
     l_wait(3, 0)
-    add_squares((4,), 0)
+    add_squares((4,), tok_l, 0)
+    project(NEAR, True, False)
     w_wait("3s")
     w_wait("4s")
-    project(near, 0, 256)
-    project(far, 0, 256)
+    project(FAR, True, True)
     inverse = lax.rsqrt(jnp.sum(squares[...], axis=1, keepdims=True) * (1.0 / DECODER_WIDTH) + EPSILON)
 
     loads[5].wait()
@@ -666,9 +678,11 @@
             pltpu.VMEM((128, 1024), BF16),
             pltpu.VMEM((512, 256), BF16),
             pltpu.VMEM((512, 256), BF16),
-            pltpu.VMEM((2048, 1024), BF16),
+            pltpu.VMEM((1024, 1024), BF16),
+            pltpu.VMEM((1024, 1024), BF16),
             pltpu.VMEM((128, 256), F32),
-            pltpu.VMEM((8192, 1280), BF16),
+            pltpu.VMEM((5120, 1280), BF16),
+            pltpu.VMEM((3072, 1280), BF16),
             pltpu.VMEM((128, 1280), BF16),
             pltpu.VMEM((256, 1280), F32),
             pltpu.VMEM((256, 128), F32),

time: 117 us -> 110 us (0.940)
  Pallas kernels: 114 us -> 107 us
    pallas_call x1, Pallas kernels: 114 us -> 107 us  [on_device(): pl.pallas_call(kernel, out_shape=jax.ShapeDtypeStruct((256, 1024), BF16),...]
where the time goes in v5:
time: 110 us
  Pallas kernels  107 us (97%)
  other arithmetic  2.13 us (2%)
    pallas_call x1, Pallas kernels, on_device(): pl.pallas_call(kernel, out_shape=jax.ShapeDtypeStruct((256, 1024), BF16),...  107 us

profile of v5, /device:TPU:1, one launch (start us, length us, event | category | flops | bytes accessed | tf_op | source)
XLA Modules:
  0.0 109.6 jit_solution(14142599636275296832)
XLA Ops:
  0.0 107.5 %shard_map.163 = bf16[256,1024]{1,0:T(8,128)(2,1)} custom-call(s32[64]{0:T(128)} %slot_ref.1, s32[64]{0:T(128)} %tenant_ref.1, s32[64]{0:T(128)} %len_ref.1, s32[8,128]{1,0:T(8,128)} %bitcast.14, s32[8,128]{1,0:T(8,128)} %bitcast.15, bf16[3,40,160]{2,1,0:T(8,128)(2,1)} %vit_qkv.1, bf16[40,160]{1,0:T(8,128)(2,1)} %bitcast.13, bf16[512,1280]{1,0:T(8,128)(2,1)} %bitcast.10, ...), custom_call_target="tpu_custom_call" | custom-call | tf_op jit(solution)/shard_map/pallas_call | solution.py:652
  107.5 2.1 %convert_element_type.3 = f32[256,1024]{1,0:T(8,128)} convert(bf16[256,1024]{1,0:T(8,128)(2,1)} %shard_map.163) | non-fusion elementwise | flops 262144 | bytes 1572864 | tf_op jit(solution)/shard_map/convert_element_type | solution.py:698

commit v6 on v5

--- a/solution.py
+++ b/solution.py
@@ -122,7 +122,7 @@
     patches_hbm, mw, w, down_hbm, up, text_hbm, perm_hbm, select_hbm, cosine_hbm, sine_hbm,
     out,
     patches, down, text, perm, select, cosine, sine, w_in, up_in,
-    g0, g1, wf, wall, pp, ln, qkv, o_all, ctx_all, enc, mwb, vis, xs, ys, tok_l, tok_e, dl, w_near, w_far, up_all, acc, squares, res,
+    g0, g1, wf, wall, pp, ln, qkv, o_all, ctx_all, enc, mwb, vis, xs, ys, tok_l, tok_e, dl, w_near, w_far, x_near, x_far, up_all, acc, squares, res,
     load_sem, gs_sem, gr_sem, fs_sem, fr_sem, ws_sem, wr_sem,
     os_sem, or_sem, ofs_sem, ofr_sem, cs_sem, cr_sem, es_sem, er_sem, ls_sem, lr_sem,
     as_sem, ar_sem, ds_sem, dr_sem,
@@ -383,15 +383,15 @@
     o_start(0, 1)
 
     g_share(1, (2, 3))
+    o_on(1, 0)
     w_start("0a")
     w_start("0b")
     w_start("0s")
     g_share(1, (1, 0))
-    o_on(1, 0)
+    o_on(1, 1)
+    o_share(0)
     g_shared(1, fr_sem)
     unpack(1)
-    o_on(1, 1)
-    o_share(0)
     for n in range(2):
         lanes = slice(256 * n, 256 * n + 256)
         qkv[:, lanes] = bdot(ln[...], wall[:, 128 + 256 * n:384 + 256 * n]).astype(BF16)
@@ -411,6 +411,8 @@
             probs = (exponent / total[None]).astype(BF16).reshape(512, 128)
             ctx_t = bdot(v_t, probs).astype(BF16)
             ctx_all[pl.ds(own_o + 80 * h, 80), 128 * q:128 * q + 128] = ctx_t[:80, :]
+        if h == 0:
+            o_on(2, 0)
 
     c_start(0, 0)
     c_start(0, 1)
@@ -424,25 +426,23 @@
             )
             enc[:, lanes] = (pp[:, lanes].astype(F32) if first else enc[:, lanes]) + term
 
-    o_on(2, 0)
     o_on(2, 1)
     o_share(1)
     project_out(t, True)
+    w_wait("0a")
+    w_start("1a")
     c_on(1, 0)
     c_on(1, 1)
-    w_wait("0a")
-    w_start("1a")
     o_shared(0)
     project_out(t - 1)
     project_out(t + 1)
     o_on(3, 0)
     o_on(3, 1)
     o_share(2)
+    w_wait("0b")
+    w_start("1b")
     c_on(2, 0)
     c_on(2, 1)
-    w_wait("0b")
-    w_start("1b")
-    w_start("1s")
     o_shared(1)
     project_out(t - 2)
     project_out(t + 2)
@@ -450,6 +450,7 @@
     o_share(3)
     c_on(3, 0)
     c_on(3, 1)
+    w_start("1s")
     o_shared(2)
     e_on(1, 0)
     e_on(1, 1)
@@ -460,11 +461,11 @@
     c_wait(3, 0)
     project_out(t + 4)
 
-    merged = jnp.zeros((128, 1024), F32)
     for j in range(4):
-        merged_in = normalize(enc[128 * j:128 * j + 128, :]).astype(BF16)
-        merged += bdot(merged_in, mwb[1280 * j:1280 * j + 1280, :])
-    vis[...] = merged.astype(BF16)
+        x_near[0:128, 1280 * j:1280 * j + 1280] = normalize(enc[128 * j:128 * j + 128, :]).astype(BF16)
+    for n in range(4):
+        lanes = slice(256 * n, 256 * n + 256)
+        vis[:, lanes] = bdot(x_near[0:128, :], mwb[:, lanes]).astype(BF16)
     e_on(2, 0)
 
     row_512 = iota((512, 128), 0)
@@ -485,8 +486,6 @@
     own_y = pl.ds(pl.multiple_of(s * 16, 16), 16)
     ys[own_y, :] = xs[own_y, :]
     e_on(2, 1)
-    w_wait("1a")
-    w_start("2a")
     e_on(3, 0)
     arrived(ys.at[pl.ds(0, 496)], ar_sem.at[0])
 
@@ -502,6 +501,8 @@
             )
     l_start(0, 0)
     l_start(0, 1)
+    w_wait("1a")
+    w_start("2a")
     w_wait("1b")
     w_start("2b")
     w_start("1c")
@@ -522,23 +523,18 @@
 
     lax.fori_loop(1, N_TP, send_down, 0)
 
-    def project(chips, late, early):
-        tops = [top for top, due in ((0, late), (128, early)) if due]
-        buf, order = (w_near, NEAR) if chips[0] in NEAR else (w_far, FAR)
-        for by, bx in chips:
-            at = chip_at(by, bx)
-            odd = lax.rem(at, 2)
-            even = (1 - odd).astype(F32).astype(BF16)
-            odd = odd.astype(F32).astype(BF16)
-            of_z = pl.ds(pl.multiple_of(at // 2 * 128, 128), 128)
-            parts = [(tok_l, tok_e)[top // 128] for top in tops]
-            parts = [part[of_z, 0:512] * even + part[of_z, 512:1024] * odd for part in parts]
-            x = jnp.concatenate(parts, axis=0) if len(parts) > 1 else parts[0]
-            rows_of = slice(tops[0], tops[-1] + 128)
-            first = order.index((by, bx)) * 512
-            for n in range(5):
-                lanes = slice(256 * n, 256 * n + 256)
-                acc[rows_of, lanes] += bdot(x, buf[first:first + 512, lanes])
+    def collect(tok, top):
+        for to, order in ((x_near, NEAR), (x_far, FAR)):
+            for n, (by, bx) in enumerate(order):
+                at = chip_at(by, bx)
+                of_z = pl.ds(pl.multiple_of(at // 2 * 128, 128), 128)
+                half = pl.ds(pl.multiple_of(lax.rem(at, 2) * 512, 512), 512)
+                to[top:top + 128, 512 * n:512 * n + 512] = tok[of_z, half]
+
+    def project(x, weight, top, size, first, last):
+        for n in range(5):
+            lanes = slice(256 * n, 256 * n + 256)
+            acc[top:top + size, lanes] += bdot(x[top:top + size, first:last], weight[first:last, lanes])
 
     def add_squares(aheads, tok, top):
         for ahead in aheads:
@@ -555,14 +551,15 @@
     e_wait(2, 1)
     e_wait(3, 0)
     add_squares(range(8), tok_e, 128)
+    collect(tok_e, 128)
     l_on(1, 1)
     add_squares((0, 1, -1), tok_l, 0)
     for name in ("0s", "1s"):
         w_wait(name)
-    project(NEAR[:5], False, True)
+    project(x_near, w_near, 128, 128, 0, 2560)
     l_on(2, 0)
     w_wait("2s")
-    project(NEAR[5:], False, True)
+    project(x_near, w_near, 128, 128, 2560, 5120)
     l_on(2, 1)
     w_wait("2a")
     w_start("3a")
@@ -582,16 +579,17 @@
     acc[...] += bdot(lora, up_all[...])
     l_wait(3, 0)
     add_squares((4,), tok_l, 0)
-    project(NEAR, True, False)
+    collect(tok_l, 0)
+    project(x_near, w_near, 0, 128, 0, 5120)
     w_wait("3s")
     w_wait("4s")
-    project(FAR, True, True)
+    project(x_far, w_far, 0, 256, 0, 3072)
     inverse = lax.rsqrt(jnp.sum(squares[...], axis=1, keepdims=True) * (1.0 / DECODER_WIDTH) + EPSILON)
 
     loads[5].wait()
     loads[6].wait()
 
-    causal = iota((128, 128), 0) >= iota((128, 128), 1)
+    causal = (iota((1024, 128), 0) & 127) >= iota((1024, 128), 1)
     ones = jnp.ones((128, 128), BF16)
     stores = []
     for l in range(2):
@@ -608,14 +606,15 @@
         key_rows = rotate(column(8)).astype(BF16)
         value_rows = jnp.concatenate([column(9).astype(BF16), ones], axis=1)
         kept = iota((128, 128), 0) < length[l]
+        queries = jnp.concatenate([rotate(column(j)).astype(BF16) for j in range(QUERY_PER_KEY)], axis=0)
+        scores = bdot_nt(queries, key_rows) * (1.0 / math.sqrt(DECODER_HEAD_DIM))
+        scores = jnp.where(causal, scores, -1e30)
+        exponent = jnp.exp(scores - jnp.max(scores, axis=1, keepdims=True)).astype(BF16)
+        summed = bdot(exponent, value_rows)
+        ratio = summed[:, :128] / summed[:, 128:]
         for j in range(QUERY_PER_KEY):
-            query = rotate(column(j)).astype(BF16)
-            scores = bdot_nt(query, key_rows) * (1.0 / math.sqrt(DECODER_HEAD_DIM))
-            scores = jnp.where(causal, scores, -1e30)
-            exponent = jnp.exp(scores - jnp.max(scores, axis=1, keepdims=True)).astype(BF16)
-            summed = bdot(exponent, value_rows)
             res[128 * l:128 * l + 128, 128 * j:128 * j + 128] = jnp.where(
-                kept, summed[:, :128] / summed[:, 128:], 0.0
+                kept, ratio[128 * j:128 * j + 128, :], 0.0
             ).astype(BF16)
         stores.append(pltpu.make_async_copy(
             res.at[pl.ds(128 * l, 128)], out.at[pl.ds(128 * l, 128)], load_sem.at[10 + l]
@@ -683,6 +682,8 @@
             pltpu.VMEM((128, 256), F32),
             pltpu.VMEM((5120, 1280), BF16),
             pltpu.VMEM((3072, 1280), BF16),
+            pltpu.VMEM((256, 5120), BF16),
+            pltpu.VMEM((256, 3072), BF16),
             pltpu.VMEM((128, 1280), BF16),
             pltpu.VMEM((256, 1280), F32),
             pltpu.VMEM((256, 128), F32),

time: 110 us -> 103 us (0.936)
  Pallas kernels: 107 us -> 101 us
    pallas_call x1, Pallas kernels: 107 us -> 101 us  [on_device(): pl.pallas_call(kernel, out_shape=jax.ShapeDtypeStruct((256, 1024), BF16),...]
where the time goes in v6:
time: 103 us
  Pallas kernels  101 us (98%)
  other arithmetic  2.13 us (2%)
    pallas_call x1, Pallas kernels, on_device(): pl.pallas_call(kernel, out_shape=jax.ShapeDtypeStruct((256, 1024), BF16),...  101 us
    convert_element_type x1, other arithmetic, on_device(): return pl.pallas_call(kernel, out_shape=jax.ShapeDtypeStruct((256, 1024),...  2.13 us

profile of v6, /device:TPU:1, one launch (start us, length us, event | category | flops | bytes accessed | tf_op | source)
XLA Modules:
  0.0 103.2 jit_solution(16339120655723892542)
XLA Ops:
  0.0 101.1 %shard_map.163 = bf16[256,1024]{1,0:T(8,128)(2,1)} custom-call(s32[64]{0:T(128)} %slot_ref.1, s32[64]{0:T(128)} %tenant_ref.1, s32[64]{0:T(128)} %len_ref.1, s32[8,128]{1,0:T(8,128)} %bitcast.14, s32[8,128]{1,0:T(8,128)} %bitcast.15, bf16[3,40,160]{2,1,0:T(8,128)(2,1)} %vit_qkv.1, bf16[40,160]{1,0:T(8,128)(2,1)} %bitcast.13, bf16[512,1280]{1,0:T(8,128)(2,1)} %bitcast.10, ...), custom_call_target="tpu_custom_call" | custom-call | tf_op jit(solution)/shard_map/pallas_call | solution.py:651
  101.1 2.1 %convert_element_type.3 = f32[256,1024]{1,0:T(8,128)} convert(bf16[256,1024]{1,0:T(8,128)(2,1)} %shard_map.163) | non-fusion elementwise | flops 262144 | bytes 1572864 | tf_op jit(solution)/shard_map/convert_element_type | solution.py:699

commit v7 on v6

--- a/solution.py
+++ b/solution.py
@@ -69,19 +69,22 @@
         "0a": [go(0, 0, part_a, ty, tx) for ty, tx in near],
         "0b": [go(0, 0, part_b, ty, tx) for ty, tx in near],
         "0s": sib([(0, 0)]),
-        "1a": [go(0, -1, part_a, 0, 1), go(-1, 0, part_a, 1, 0)]
+        "1a": [go(0, -1, (0, 64), 0, 1), go(0, 1, (64, 64), 0, -1)]
         + [go(0, side, part_a, to, 0) for side in sides for to in sides],
-        "1b": [go(1, 0, part_b, -1, 0)]
+        "1b": [go(-1, 0, (128, 64), 1, 0), go(1, 0, (192, 64), -1, 0)]
         + [go(side, 0, part_b, 0, to) for side in sides for to in sides],
-        "1c": [go(0, 1, (128, 64), 0, -1), go(0, -1, (192, 64), 0, 1)],
+        "1c": [
+            go(0, 1, (128, 64), 0, -1), go(0, -1, (192, 64), 0, 1), go(-1, 0, (0, 64), 1, 0), go(1, 0, (64, 64), -1, 0),
+        ],
         "1s": sib(near),
         "2a": [go(0, 2, part_a, 1, 0), go(0, 2, part_a, -1, 0), go(-1, 1, part_a, 1, 0), go(1, -1, part_a, -1, 0)],
         "2b": [go(2, 0, part_b, 0, 1), go(2, 0, part_b, 0, -1), go(1, -1, part_b, 0, 1), go(-1, 1, part_b, 0, -1)],
-        "2s": sib([(2, 0), (-1, -1), (-1, 1), (1, -1), (1, 1)]),
+        "2s": sib([(-1, -1), (-1, 1), (1, -1), (1, 1)]),
         "3a": [go(-1, 2, (0, 64), 1, 0), go(1, 2, (64, 64), -1, 0)],
         "3b": [go(2, -1, (128, 64), 0, 1), go(2, 1, (192, 64), 0, -1)],
         "3s": sib([(-1, 2), (1, 2), (2, -1), (2, 1)]),
-        "4s": sib([(0, 2), (2, 2)]),
+        "4s": sib([(0, 2), (2, 0)]),
+        "5s": sib([(2, 2)]),
     }
     return {
         name: (i, sum(entry[3] for entry in entries), entries) for i, (name, entries) in enumerate(lists.items())
@@ -89,8 +92,8 @@
 
 
 W_GROUPS = plane_copies()
-NEAR = [(0, 0), (0, 3), (0, 1), (3, 0), (1, 0), (2, 0), (3, 3), (3, 1), (1, 3), (1, 1)]
-FAR = [(3, 2), (1, 2), (2, 3), (2, 1), (0, 2), (2, 2)]
+NEAR = [(0, 0), (0, 3), (0, 1), (3, 0), (1, 0), (3, 3), (3, 1), (1, 3), (1, 1)]
+FAR = [(3, 2), (1, 2), (2, 3), (2, 1), (0, 2), (2, 0), (2, 2)]
 LANES = (256, 384)
 
 
@@ -363,6 +366,7 @@
 
     g_share(0, (2, 3, 1, 0))
     g_start(1)
+    e_on(1, 0)
     g_shared(0, fr_sem)
 
     def unpack(phase):
@@ -452,8 +456,8 @@
     c_on(3, 1)
     w_start("1s")
     o_shared(2)
-    e_on(1, 0)
     e_on(1, 1)
+    e_on(2, 0)
     project_out(t - 3)
     project_out(t + 3)
     o_shared(3)
@@ -466,7 +470,7 @@
     for n in range(4):
         lanes = slice(256 * n, 256 * n + 256)
         vis[:, lanes] = bdot(x_near[0:128, :], mwb[:, lanes]).astype(BF16)
-    e_on(2, 0)
+    e_on(2, 1)
 
     row_512 = iota((512, 128), 0)
     outgoing = jnp.zeros((512, 256), F32)
@@ -485,9 +489,14 @@
     lax.fori_loop(1, N_SEQ, send_rows, 0)
     own_y = pl.ds(pl.multiple_of(s * 16, 16), 16)
     ys[own_y, :] = xs[own_y, :]
-    e_on(2, 1)
     e_on(3, 0)
+    w_wait("1a")
+    w_wait("1b")
     arrived(ys.at[pl.ds(0, 496)], ar_sem.at[0])
+    w_start("2a")
+    w_start("2b")
+    w_start("1c")
+    w_start("2s")
 
     row_128 = iota((128, 512), 0)
     position = iota((64, 256), 0)
@@ -501,12 +510,6 @@
             )
     l_start(0, 0)
     l_start(0, 1)
-    w_wait("1a")
-    w_start("2a")
-    w_wait("1b")
-    w_start("2b")
-    w_start("1c")
-    w_start("2s")
 
     loads[4].wait()
     own_rows = jnp.concatenate([tok_l[pl.ds(own_tok, 128), :], tok_e[pl.ds(own_tok, 128), :]], axis=0)
@@ -559,20 +562,22 @@
     project(x_near, w_near, 128, 128, 0, 2560)
     l_on(2, 0)
     w_wait("2s")
-    project(x_near, w_near, 128, 128, 2560, 5120)
+    project(x_near, w_near, 128, 128, 2560, 4608)
     l_on(2, 1)
     w_wait("2a")
     w_start("3a")
-    add_squares((2, -2), tok_l, 0)
-    l_on(3, 0)
     w_wait("2b")
     w_start("3b")
     w_start("3s")
+    add_squares((2, -2), tok_l, 0)
+    l_on(3, 0)
     l_on(3, 1)
     add_squares((3, -3), tok_l, 0)
-    for name in ("1c", "3a", "3b"):
-        w_wait(name)
+    w_wait("1c")
     w_start("4s")
+    w_wait("3a")
+    w_wait("3b")
+    w_start("5s")
     arrived(dl.at[pl.ds(0, 112)], dr_sem.at[0])
     down_t = jnp.sum(dl[...].reshape(8, 16, 256), axis=0)
     lora = jnp.transpose(jnp.concatenate([down_t] * 8, axis=0) * tenant_mask).astype(BF16)
@@ -580,10 +585,11 @@
     l_wait(3, 0)
     add_squares((4,), tok_l, 0)
     collect(tok_l, 0)
-    project(x_near, w_near, 0, 128, 0, 5120)
+    project(x_near, w_near, 0, 128, 0, 4608)
     w_wait("3s")
     w_wait("4s")
-    project(x_far, w_far, 0, 256, 0, 3072)
+    w_wait("5s")
+    project(x_far, w_far, 0, 256, 0, 3584)
     inverse = lax.rsqrt(jnp.sum(squares[...], axis=1, keepdims=True) * (1.0 / DECODER_WIDTH) + EPSILON)
 
     loads[5].wait()
@@ -680,10 +686,10 @@
             pltpu.VMEM((1024, 1024), BF16),
             pltpu.VMEM((1024, 1024), BF16),
             pltpu.VMEM((128, 256), F32),
-            pltpu.VMEM((5120, 1280), BF16),
-            pltpu.VMEM((3072, 1280), BF16),
+            pltpu.VMEM((4608, 1280), BF16),
+            pltpu.VMEM((3584, 1280), BF16),
             pltpu.VMEM((256, 5120), BF16),
-            pltpu.VMEM((256, 3072), BF16),
+            pltpu.VMEM((256, 3584), BF16),
             pltpu.VMEM((128, 1280), BF16),
             pltpu.VMEM((256, 1280), F32),
             pltpu.VMEM((256, 128), F32),

time: 103 us -> 100 us (0.971)
  Pallas kernels: 101 us -> 97.8 us
    pallas_call x1, Pallas kernels: 101 us -> 97.8 us  [on_device(): pl.pallas_call(kernel, out_shape=jax.ShapeDtypeStruct((256, 1024), BF16),...]
where the time goes in v7:
time: 100 us
  Pallas kernels  97.8 us (98%)
  other arithmetic  2.13 us (2%)
    pallas_call x1, Pallas kernels, on_device(): pl.pallas_call(kernel, out_shape=jax.ShapeDtypeStruct((256, 1024), BF16),...  97.8 us
    convert_element_type x1, other arithmetic, on_device(): return pl.pallas_call(kernel, out_shape=jax.ShapeDtypeStruct((256, 1024),...  2.13 us

profile of v7, /device:TPU:1, one launch (start us, length us, event | category | flops | bytes accessed | tf_op | source)
XLA Modules:
  0.0 100.0 jit_solution(16753473246662567020)
XLA Ops:
  0.0 97.8 %shard_map.163 = bf16[256,1024]{1,0:T(8,128)(2,1)} custom-call(s32[64]{0:T(128)} %slot_ref.1, s32[64]{0:T(128)} %tenant_ref.1, s32[64]{0:T(128)} %len_ref.1, s32[8,128]{1,0:T(8,128)} %bitcast.14, s32[8,128]{1,0:T(8,128)} %bitcast.15, bf16[3,40,160]{2,1,0:T(8,128)(2,1)} %vit_qkv.1, bf16[40,160]{1,0:T(8,128)(2,1)} %bitcast.13, bf16[512,1280]{1,0:T(8,128)(2,1)} %bitcast.10, ...), custom_call_target="tpu_custom_call" | custom-call | tf_op jit(solution)/shard_map/pallas_call | solution.py:657
  97.8 2.1 %convert_element_type.3 = f32[256,1024]{1,0:T(8,128)} convert(bf16[256,1024]{1,0:T(8,128)(2,1)} %shard_map.163) | non-fusion elementwise | flops 262144 | bytes 1572864 | tf_op jit(solution)/shard_map/convert_element_type | solution.py:705

commit v8 on v7

--- a/solution.py
+++ b/solution.py
@@ -524,7 +524,6 @@
         ).start()
         return carry
 
-    lax.fori_loop(1, N_TP, send_down, 0)
 
     def collect(tok, top):
         for to, order in ((x_near, NEAR), (x_far, FAR)):
@@ -571,6 +570,7 @@
     w_start("3s")
     add_squares((2, -2), tok_l, 0)
     l_on(3, 0)
+    lax.fori_loop(1, N_TP, send_down, 0)
     l_on(3, 1)
     add_squares((3, -3), tok_l, 0)
     w_wait("1c")
@@ -578,10 +578,6 @@
     w_wait("3a")
     w_wait("3b")
     w_start("5s")
-    arrived(dl.at[pl.ds(0, 112)], dr_sem.at[0])
-    down_t = jnp.sum(dl[...].reshape(8, 16, 256), axis=0)
-    lora = jnp.transpose(jnp.concatenate([down_t] * 8, axis=0) * tenant_mask).astype(BF16)
-    acc[...] += bdot(lora, up_all[...])
     l_wait(3, 0)
     add_squares((4,), tok_l, 0)
     collect(tok_l, 0)
@@ -590,6 +586,10 @@
     w_wait("4s")
     w_wait("5s")
     project(x_far, w_far, 0, 256, 0, 3584)
+    arrived(dl.at[pl.ds(0, 112)], dr_sem.at[0])
+    down_t = jnp.sum(dl[...].reshape(8, 16, 256), axis=0)
+    lora = jnp.transpose(jnp.concatenate([down_t] * 8, axis=0) * tenant_mask).astype(BF16)
+    acc[...] += bdot(lora, up_all[...])
     inverse = lax.rsqrt(jnp.sum(squares[...], axis=1, keepdims=True) * (1.0 / DECODER_WIDTH) + EPSILON)
 
     loads[5].wait()

time: 100 us -> 98.6 us (0.986)
  Pallas kernels: 97.8 us -> 96.3 us
    pallas_call x1, Pallas kernels: 97.8 us -> 96.3 us  [on_device(): pl.pallas_call(kernel, out_shape=jax.ShapeDtypeStruct((256, 1024), BF16),...]
where the time goes in v8:
time: 98.6 us; the launch traced here: 98.4 us
  Pallas kernels  96.3 us (98%)
  other arithmetic  2.13 us (2%)
    pallas_call x1, Pallas kernels, on_device(): pl.pallas_call(kernel, out_shape=jax.ShapeDtypeStruct((256, 1024), BF16),...  96.3 us
    convert_element_type x1, other arithmetic, on_device(): return pl.pallas_call(kernel, out_shape=jax.ShapeDtypeStruct((256, 1024),...  2.13 us

profile of v8, /device:TPU:1, one launch (start us, length us, event | category | flops | bytes accessed | tf_op | source)
XLA Modules:
  0.0 98.4 jit_solution(5353402962752543347)
XLA Ops:
  0.0 96.3 %shard_map.163 = bf16[256,1024]{1,0:T(8,128)(2,1)} custom-call(s32[64]{0:T(128)} %slot_ref.1, s32[64]{0:T(128)} %tenant_ref.1, s32[64]{0:T(128)} %len_ref.1, s32[8,128]{1,0:T(8,128)} %bitcast.14, s32[8,128]{1,0:T(8,128)} %bitcast.15, bf16[3,40,160]{2,1,0:T(8,128)(2,1)} %vit_qkv.1, bf16[40,160]{1,0:T(8,128)(2,1)} %bitcast.13, bf16[512,1280]{1,0:T(8,128)(2,1)} %bitcast.10, ...), custom_call_target="tpu_custom_call" | custom-call | tf_op jit(solution)/shard_map/pallas_call | solution.py:657
  96.3 2.1 %convert_element_type.3 = f32[256,1024]{1,0:T(8,128)} convert(bf16[256,1024]{1,0:T(8,128)(2,1)} %shard_map.163) | non-fusion elementwise | flops 262144 | bytes 1572864 | tf_op jit(solution)/shard_map/convert_element_type | solution.py:705
